TPU v7x, 32 devices: a whole 2x2x4 slice. The times are simulated.
32 devices in a mesh: dp: 4 (over y, x), feat: 2 (over core), cent: 4 (over z).
Axes of the slice: x: 2, y: 2, z: 4, core: 2. Of those that a mesh axis runs over, the one named last changes fastest.
Arguments:
- embeddings: bfloat16 [4096, 768], P(('dp', 'cent')), may hold values from -12 to 12
- projection: bfloat16 [768, 8192], P(None, 'feat'), may hold values from -0.21875 to 0.21875
- phases: float32 [8192], P('feat'), may hold values from -4 to 4
- centroids: bfloat16 [4096, 8192], P('cent', 'feat'), may hold values from -7 to 7
Outputs:
- updated: float32 [4096, 8192], P('cent', 'feat')
All inputs are finite; a program needn't handle non-finite values.
Results may differ from a plain program's by a relative error of at most 0.0003.
Values may be sent and summed in bfloat16 or wider, within the bound.
A program may use at most 192 MiB of HBM per device.

v0:
```python
import math

import jax
import jax.numpy as jnp
from jax import lax
from jax.sharding import PartitionSpec as P

F = 8192


SQRT_TWO = math.sqrt(2.0)
SHARP_FACTOR = 1.5
PRIOR_MASS = 1.0


def featurize(embeddings, projection, phases):
    projected = jnp.dot(embeddings, projection, preferred_element_type=jnp.float32)
    return (SQRT_TWO * jnp.cos(projected + phases)).astype(jnp.bfloat16)


def score_part(features, centers):
    center_wide = centers.astype(jnp.float32)
    center_sq = jnp.sum(center_wide * center_wide, axis=1)
    inner_part = lax.dot_general(
        features, centers, (((1,), (1,)), ((), ())), preferred_element_type=jnp.float32
    )
    return 2.0 * inner_part - center_sq[None, :]


def row_contract(weights, features):
    return lax.dot_general(
        weights, features, (((0,), (0,)), ((), ())), preferred_element_type=jnp.float32
    )


def local_softmax(logits):
    top_score = jnp.max(logits, axis=1, keepdims=True)
    exp_terms = jnp.exp(logits - top_score)
    return (exp_terms / jnp.sum(exp_terms, axis=1, keepdims=True)).astype(jnp.bfloat16)


def responsibilities(partial_value, sharpness, normalize):
    return normalize(sharpness * lax.psum(partial_value, "feat"))


def shards(embeddings, projection, phases, centroids):
    features = featurize(embeddings, projection, phases)
    sharpness = SHARP_FACTOR / math.sqrt(F)
    local_rows = features.shape[0]
    local_cent = centroids.shape[0]
    n_data = lax.axis_size("dp")
    n_groups = lax.axis_size("cent")
    partial_value = score_part(features, lax.all_gather(centroids, "cent", axis=0, tiled=True))
    resp = responsibilities(partial_value, sharpness, local_softmax)
    block_rows = local_cent // n_data
    total_cent = resp.shape[1]
    reordered = (
        resp.reshape(local_rows, n_groups, n_data, block_rows)
        .transpose(0, 2, 1, 3)
        .reshape(local_rows, total_cent)
    )
    sums_block, mass_block = lax.psum_scatter(
        (row_contract(reordered, features), jnp.sum(reordered.astype(jnp.float32), axis=0)),
        ("dp", "cent"),
        scatter_dimension=0,
        tiled=True,
    )
    old_block = lax.dynamic_slice_in_dim(
        centroids, lax.axis_index("dp") * block_rows, block_rows, 0
    ).astype(jnp.float32)
    fresh_block = (sums_block + PRIOR_MASS * old_block) / (mass_block + PRIOR_MASS)[:, None]
    updated = lax.all_gather(fresh_block, "dp", axis=0, tiled=True)
    return updated


def solution(mesh):
    return jax.shard_map(
        shards,
        mesh=mesh,
        in_specs=(P(("dp", "cent"), None), P(None, "feat"), P("feat"), P("cent", "feat")),
        out_specs=P("cent", "feat"),
        check_vma=False,
    )
```

profile of v0, /device:TPU:0, one launch (start us, length us, event | category | flops | bytes accessed | tf_op | source)
XLA Modules:
  0.0 2215.8 jit_solution(16581665132473078666)
XLA Ops:
  6.5 0.0 copy-start
  6.5 0.0 copy-start.4
  6.5 0.0 all-gather.3.cloned.1.call-start
  6.5 0.7 all-gather.3.cloned.1.call-update
  7.3 0.0 all-reduce.3.cloned.1.call-start
  7.3 0.2 copy-done
  7.5 0.0 copy-done.4
  7.5 16.7 fusion.3
  24.2 0.0 copy-start.3
  24.2 548.9 %all-gather.3.cloned.1.call-done = bf16[4096,4096]{1,0:T(8,128)(2,1)} async-done(((bf16[1024,4096]{1,0:T(8,128)(2,1)}), bf16[4096,4096]{1,0:T(8,128)(2,1)}) %all-gather.3.cloned.1.call-update) | async-done | bytes 33554448 | tf_op jit(solution)/shard_map/all_gather | solution.py:53
  573.1 11.3 multiply_reduce_fusion
  584.4 0.0 copy-done.3
  584.4 16.6 fusion
  601.0 0.0 all-reduce.3.cloned.1.call-update
  601.1 0.2 reduce-scatter.2.cloned.1.call-start
  601.3 26.5 %all-reduce.3.cloned.1.call-done = f32[256,4096]{1,0:T(8,128)} async-done(((f32[256,4096]{1,0:T(8,128)}), f32[256,4096]{1,0:T(8,128)}) %all-reduce.3.cloned.1.call-update) | async-done | bytes 4194320 | tf_op jit(solution)/shard_map/psum | solution.py:43
  627.8 0.0 copy-start.2
  627.8 2.7 multiply_reduce_fusion.1
  630.5 0.7 copy-done.2
  631.3 0.8 fusion.4
  632.1 1.0 divide_convert_fusion
  633.0 2.8 reshape.12
  635.8 3.0 copy.6
  638.8 25.5 %fusion.5 = f32[4096,4096]{1,0:T(8,128)} fusion(bf16[256,4096]{0,1:T(8,128)(2,1)S(1)} %bitcast.13, bf16[256,4096]{1,0:T(8,128)(2,1)} %copy-done.3), kind=kOutput, calls=%fused_computation.14 | convolution fusion | flops 8589934592 | bytes 71303168 | tf_op jit(solution)/shard_map/dot_general | solution.py:31
  664.3 0.0 copy-start.5
  664.3 0.0 reduce-scatter.2.cloned.1.call-update
  664.4 0.0 all-gather.5.cloned.1.call-start
  664.4 0.6 copy-done.5
  665.0 0.6 dynamic-slice
  666.2 0.6 convert_reduce_fusion
  666.9 81.9 %all-reduce = f32[4096]{0:T(1024)S(1)} all-reduce(f32[4096]{0:T(1024)S(1)} %bitcast.15), channel_id=3, replica_groups=mesh['dp'=4,'feat'=2,'cent'=4] {'dp','cent'}, use_global_device_ids=true, to_apply=%region_6.0.clone | all-reduce | flops 4096 | bytes 32768
  748.8 0.1 dynamic-slice_add_fusion
  748.9 1285.4 %reduce-scatter.2.cloned.1.call-done = f32[256,4096]{1,0:T(8,128)} async-done(((f32[4096,4096]{1,0:T(8,128)}), f32[256,4096]{1,0:T(8,128)}) %reduce-scatter.2.cloned.1.call-update) | async-done | bytes 4194320 | tf_op jit(solution)/shard_map/reduce_scatter | solution.py:62
  2034.2 5.7 add_divide_fusion
  2039.9 0.0 all-gather.5.cloned.1.call-update
  2039.9 157.5 %all-gather.5.cloned.1.call-done = f32[1024,4096]{1,0:T(8,128)} async-done(((f32[256,4096]{1,0:T(8,128)}), f32[1024,4096]{1,0:T(8,128)}) %all-gather.5.cloned.1.call-update) | async-done | bytes 16777232 | tf_op jit(solution)/shard_map/all_gather | solution.py:72
  2197.5 0.0 copy-start.1
  2197.5 11.8 copy.10
  2209.2 0.0 copy-done.1
  (1 shorter events, 0.0 us)
Async XLA Ops:
  6.5 1.0 copy-start
  6.5 1.0 copy-start.4
  6.5 566.6 %all-gather.3.cloned.1.call-start = ((), (), s32[]{:S(2)}) async-start(), calls=%async_computation.1 | async-start | bytes 41943040 | tf_op jit(solution)/shard_map/all_gather | solution.py:53
  7.3 620.5 %all-reduce.3.cloned.1.call-start = ((), (), s32[]{:S(2)}) async-start(), calls=%async_computation.2 | async-start | bytes 8388608 | tf_op jit(solution)/shard_map/psum | solution.py:43
  24.2 560.2 %copy-start.3 = (bf16[256,4096]{1,0:T(8,128)(2,1)}, bf16[256,4096]{1,0:T(8,128)(2,1)S(1)}, u32[]{:S(2)}) copy-start(bf16[256,4096]{1,0:T(8,128)(2,1)S(1)} %fusion.3) | copy-start | bytes 6291460
  601.1 1433.2 %reduce-scatter.2.cloned.1.call-start = ((), (), s32[]{:S(2)}) async-start(), calls=%async_computation.3 | async-start | bytes 71303168 | tf_op jit(solution)/shard_map/reduce_scatter | solution.py:62
  627.8 3.4 copy-start.2
  664.3 0.7 copy-start.5
  664.4 1533.1 %all-gather.5.cloned.1.call-start = ((), (), s32[]{:S(2)}) async-start(), calls=%async_computation.4 | async-start | bytes 20971520 | tf_op jit(solution)/shard_map/all_gather | solution.py:72
  2197.5 11.8 copy-start.1
Sparse Core Ops, SparseCore 0:
  8.9 564.1 all-gather.2
  601.2 26.5 all-reduce.2
  664.5 1369.6 reduce-scatter.1
  2040.1 157.3 all-gather.4
where the time goes:
time: 2220 us
  waiting for transfers between devices  2020 us (91%)
  blocking collectives  81.9 us (4%)
  matrix products  58.8 us (3%)
  other arithmetic  22.3 us (1%)
    reduce_scatter x1, waiting for transfers between devices, shards(): lax.psum_scatter((row_contract(reordered, features), jnp.sum(reordered.as...  1290 us
    all_gather x1, waiting for transfers between devices, shards(): lax.all_gather(centroids, 'cent', axis=0, tiled=True)  549 us
    all_gather x1, waiting for transfers between devices, shards(): updated = lax.all_gather(fresh_block, 'dp', axis=0, tiled=True)  158 us
    unnamed x1, blocking collectives  81.9 us
  transfers between devices with their start and end apart: 4, of which 4 were waited for; matrix products, arithmetic and copies ran while one was open for 1% of the time, Pallas kernels for 0%

commit v1 on v0

v1 whole, which is shorter than its diff:
```python
import functools
import math

import jax
import jax.numpy as jnp
from jax import lax
from jax.experimental import pallas as pl
from jax.experimental.pallas import tpu as pltpu
from jax.sharding import PartitionSpec as P

F = 8192
SHARP_FACTOR = 1.5
PRIOR_MASS = 1.0

COS_COEFS = (
    1.4142135468471868,
    -0.7071066266011933,
    0.058925313538275806,
    -0.0019640317236862027,
    3.502984094725661e-05,
    -3.829489560381237e-07,
    2.4385896105334273e-09,
)
INV_TURN = 1.0 / (2.0 * math.pi)
TURN_HI = 6.28125
TURN_LO = 2.0 * math.pi - TURN_HI


def scaled_cos(x):
    turns = jnp.round(x * INV_TURN)
    r = (x - turns * TURN_HI) - turns * TURN_LO
    u = r * r
    y = COS_COEFS[-1]
    for c in COS_COEFS[-2::-1]:
        y = y * u + c
    return y


def feature_kernel(sub_rows, sub_cols, e_ref, p_ref, b_ref, o_ref):
    rows, cols = o_ref.shape
    for j in range(cols // sub_cols):
        cs = slice(j * sub_cols, (j + 1) * sub_cols)
        for i in range(rows // sub_rows):
            rs = slice(i * sub_rows, (i + 1) * sub_rows)
            x = jnp.dot(e_ref[rs, :], p_ref[:, cs], preferred_element_type=jnp.float32)
            o_ref[rs, cs] = scaled_cos(x + b_ref[:, cs]).astype(jnp.bfloat16)


def featurize(embeddings, projection, phases):
    rows, width = embeddings.shape
    cols = projection.shape[1]
    tr, tc = min(512, rows), min(1024, cols)
    return pl.pallas_call(
        functools.partial(feature_kernel, min(256, tr), min(256, tc)),
        grid=(cols // tc, rows // tr),
        in_specs=[
            pl.BlockSpec((tr, width), lambda j, i: (i, 0)),
            pl.BlockSpec((width, tc), lambda j, i: (0, j)),
            pl.BlockSpec((1, tc), lambda j, i: (0, j)),
        ],
        out_specs=pl.BlockSpec((tr, tc), lambda j, i: (i, j)),
        out_shape=jax.ShapeDtypeStruct((rows, cols), jnp.bfloat16),
        compiler_params=pltpu.CompilerParams(vmem_limit_bytes=32 << 20),
        cost_estimate=pl.CostEstimate(
            flops=2 * rows * width * cols,
            bytes_accessed=2 * (rows * cols + rows * width + width * cols),
            transcendentals=rows * cols,
        ),
        name="featurize",
    )(embeddings, projection, phases.reshape(1, cols))


def sums_kernel(r_ref, f_ref, c_ref, m_ref, o_ref):
    groups, _, depth = r_ref.shape
    total = None
    for g in range(groups):
        part = jnp.dot(
            r_ref[g],
            f_ref[g * depth : (g + 1) * depth, :],
            preferred_element_type=jnp.float32,
        )
        total = part if total is None else total + part
    o_ref[...] = (total + PRIOR_MASS * c_ref[...].astype(jnp.float32)) / (
        m_ref[...] + PRIOR_MASS
    )


def update(resp, features, centroids, mass):
    groups, cents, depth = resp.shape
    rows, cols = features.shape
    tk, tc = min(512, cents), min(512, cols)
    return pl.pallas_call(
        sums_kernel,
        grid=(cents // tk, cols // tc),
        in_specs=[
            pl.BlockSpec((groups, tk, depth), lambda i, j: (0, i, 0)),
            pl.BlockSpec((rows, tc), lambda i, j: (0, j)),
            pl.BlockSpec((tk, tc), lambda i, j: (i, j)),
            pl.BlockSpec((tk, 1), lambda i, j: (i, 0)),
        ],
        out_specs=pl.BlockSpec((tk, tc), lambda i, j: (i, j)),
        out_shape=jax.ShapeDtypeStruct((cents, cols), jnp.float32),
        compiler_params=pltpu.CompilerParams(vmem_limit_bytes=48 << 20),
        cost_estimate=pl.CostEstimate(
            flops=2 * rows * cents * cols,
            bytes_accessed=2 * (rows * cols + rows * cents) + 6 * cents * cols,
            transcendentals=0,
        ),
        name="update",
    )(resp, features, centroids, mass)


def my_part(x, axis_name):
    size = x.shape[0] // lax.axis_size(axis_name)
    return lax.dynamic_slice_in_dim(x, lax.axis_index(axis_name) * size, size, 0)


def shards(embeddings, projection, phases, centroids):
    sharpness = SHARP_FACTOR / math.sqrt(F)
    own = lax.all_gather(my_part(embeddings, "feat"), ("cent", "feat"), axis=0, tiled=True)
    every = lax.all_gather(my_part(own, "feat"), ("dp", "feat"), axis=0, tiled=True)
    wide = centroids.astype(jnp.float32)
    center_sq = jnp.sum(wide * wide, axis=1)
    own_features = featurize(own, projection, phases)
    inner = lax.dot_general(
        centroids, own_features, (((1,), (1,)), ((), ())), preferred_element_type=jnp.float32
    )
    partial_value = 2.0 * inner - center_sq[:, None]
    logits = sharpness * lax.psum_scatter(
        partial_value, "feat", scatter_dimension=1, tiled=True
    )
    top = jnp.max(logits, axis=0)
    local_sum = jnp.sum(jnp.exp(logits - top[None, :]), axis=0)
    stats = lax.all_gather(jnp.stack([top, local_sum]), "cent", axis=0, tiled=False)
    peak = jnp.max(stats[:, 0], axis=0)
    norm = jnp.sum(stats[:, 1] * jnp.exp(stats[:, 0] - peak[None, :]), axis=0)
    resp = (jnp.exp(logits - peak[None, :]) / norm[None, :]).astype(jnp.bfloat16)
    all_resp = lax.all_gather(resp, ("dp", "feat"), axis=0, tiled=False)
    features = featurize(every, projection, phases)
    mass = jnp.sum(all_resp.astype(jnp.float32), axis=(0, 2))
    return update(all_resp, features, centroids, mass[:, None])


def solution(mesh):
    return jax.shard_map(
        shards,
        mesh=mesh,
        in_specs=(P(("dp", "cent"), None), P(None, "feat"), P("feat"), P("cent", "feat")),
        out_specs=P("cent", "feat"),
        check_vma=False,
    )
```

time: 2220 us -> 281 us (0.13)
  waiting for transfers between devices: 2020 us -> 62.3 us
  Pallas kernels: 0 us -> 137 us
  blocking collectives: 81.9 us -> 13.7 us
  matrix products: 58.8 us -> 12.6 us
    reduce_scatter x1, waiting for transfers between devices: 1290 us -> 9.28 us  [shards(): lax.psum_scatter(partial_value, 'feat', scatter_dimension=1, tiled=True)]
    all_gather x2 -> x3, waiting for transfers between devices: 706 us -> 52.9 us  [the longest x1 29.5 us: shards(): lax.all_gather(my_part(own, 'feat'), ('dp', 'feat'), axis=0, tiled=True)]
    pallas_call x0 -> x3, Pallas kernels: none -> 137 us  [the longest x2 90.8 us: featurize(): pl.pallas_call(functools.partial(feature_kernel, min(256, tr), min(256, t...]
    unnamed x1 -> x0, blocking collectives: 81.9 us -> none
    dot_general x3 -> x1, matrix products: 58.8 us -> 12.6 us  [shards(): lax.dot_general(centroids, own_features, (((1,), (1,)), ((), ())), prefer...]
    psum x1 -> x0, waiting for transfers between devices: 26.5 us -> none  [responsibilities(): return normalize(sharpness * lax.psum(partial_value, 'feat'))]
  transfers between devices with their start and end apart: 4 -> 4, of which waited for: 4 -> 3; matrix products, arithmetic and copies ran while one was open for 1% -> 4% of each run, Pallas kernels for 0% -> 26%
where the time goes in v1:
time: 281 us; the launch traced here: 280 us
  Pallas kernels  137 us (49%)
  waiting for transfers between devices  62.3 us (22%)
  local copies, waits for them, and re-layouts  26 us (9%)
  other arithmetic  15.2 us (5%)
  blocking collectives  13.7 us (5%)
  between operations  13.2 us (5%)
  matrix products  12.6 us (4%)
    pallas_call x2, Pallas kernels, featurize(): pl.pallas_call(functools.partial(feature_kernel, min(256, tr), min(256, t...  90.8 us
    pallas_call x1, Pallas kernels, update(): pl.pallas_call(sums_kernel, grid=(cents // tk, cols // tc), in_specs=[pl....  46.2 us
    all_gather x1, waiting for transfers between devices, shards(): lax.all_gather(my_part(own, 'feat'), ('dp', 'feat'), axis=0, tiled=True)  29.5 us
    all_gather x1, waiting for transfers between devices, shards(): lax.all_gather(my_part(embeddings, 'feat'), ('cent', 'feat'), axis=0, til...  23.4 us
    all_gather x1, blocking collectives, shards(): lax.all_gather(jnp.stack([top, local_sum]), 'cent', axis=0, tiled=False)  13.7 us
    dot_general x1, matrix products, shards(): lax.dot_general(centroids, own_features, (((1,), (1,)), ((), ())), prefer...  12.6 us
    unnamed x18, local copies, waits for them, and re-layouts  12.1 us
    all_gather x1, local copies, waits for them, and re-layouts, shards(): all_resp = lax.all_gather(resp, ('dp', 'feat'), axis=0, tiled=False)  12 us
  transfers between devices with their start and end apart: 4, of which 3 were waited for; matrix products, arithmetic and copies ran while one was open for 4% of the time, Pallas kernels for 26%

profile of v1, /device:TPU:0, one launch (start us, length us, event | category | flops | bytes accessed | tf_op | source)
XLA Modules:
  0.0 280.1 jit_solution(14886720341760126288)
XLA Ops:
  6.5 0.0 copy-start
  6.5 0.0 all-gather.7.cloned.1.call-start
  6.5 1.0 copy-done
  7.5 0.7 constant_dynamic-slice_fusion.1
  8.2 0.0 all-gather.7.cloned.1.call-update
  8.2 0.0 copy-start.7
  8.3 0.0 reduce-scatter.2.cloned.1.call-start
  8.3 5.1 %multiply_reduce_fusion = f32[1024]{0:T(1024)S(1)} fusion(bf16[1024,4096]{1,0:T(8,128)(2,1)} %c_ref.1), kind=kLoop, calls=%fused_computation.1 | loop fusion | flops 12581888 | bytes 8392704 | tf_op jit(solution)/shard_map/reduce_sum | solution.py:123
  13.4 23.4 %all-gather.7.cloned.1.call-done.e_ref = bf16[1024,768]{1,0:T(8,128)(2,1)} async-done(((bf16[128,768]{1,0:T(8,128)(2,1)}), bf16[1024,768]{1,0:T(8,128)(2,1)}) %all-gather.7.cloned.1.call-update) | async-done | bytes 1572880 | tf_op jit(solution)/shard_map/all_gather | solution.py:120
  36.8 0.0 copy-done.7
  36.8 0.0 copy-start.2
  36.8 1.4 copy-done.2
  38.2 0.0 copy-start.4
  38.2 2.8 copy-done.4
  41.0 18.5 %featurize.2 = bf16[1024,4096]{1,0:T(8,128)(2,1)S(1)} custom-call(bf16[1024,768]{1,0:T(8,128)(2,1)S(1)} %copy-done.2, bf16[768,4096]{1,0:T(8,128)(2,1)S(1)} %copy-done.4, f32[1,4096]{1,0:T(1,128)S(1)} %bitcast.23), custom_call_target="tpu_custom_call" | custom-call | flops 6442450944 | bytes 16252928 | tf_op jit(solution)/shard_map/featurize/pallas_call | solution.py:53
  59.5 12.6 %subtract_bitcast_fusion = f32[1024,1024]{0,1:T(8,128)} fusion(bf16[1024,4096]{1,0:T(8,128)(2,1)S(1)} %featurize.2, bf16[1024,4096]{1,0:T(8,128)(2,1)} %c_ref.1, f32[1024]{0:T(1024)S(1)} %multiply_reduce_fusion), kind=kOutput, calls=%fused_computation.2 | convolution fusion | flops 8592031744 | bytes 20975616 | tf_op jit(solution)/shard_map/dot_general | solution.py:125
  72.1 0.0 copy-start.3
  72.1 0.0 reduce-scatter.2.cloned.1.call-update
  72.1 0.0 all-gather.9.cloned.1.call-start
  72.2 1.3 copy-done.3
  73.5 1.0 constant_dynamic-slice_fusion
  74.5 0.0 all-gather.9.cloned.1.call-update
  74.5 0.0 all-gather.11.cloned.1.call-start
  74.6 9.3 %reduce-scatter.2.cloned.1.call-done = f32[1024,512]{0,1:T(8,128)} async-done(((f32[1024,1024]{0,1:T(8,128)}), f32[1024,512]{0,1:T(8,128)}) %reduce-scatter.2.cloned.1.call-update) | async-done | bytes 2097168 | tf_op jit(solution)/shard_map/reduce_scatter | solution.py:129
  83.9 0.0 copy-start.8
  83.9 2.0 multiply_reduce_fusion.1
  85.8 2.1 exponential_reduce_fusion
  87.9 13.7 %all-gather.2 = f32[4,2,512]{2,1,0:T(2,128)S(1)} all-gather(f32[1,2,512]{2,1,0:T(2,128)S(1)} %maximum_bitcast_fusion), channel_id=2, replica_groups=mesh['dp'=4,'feat'=2,'cent'=4] {'cent'}, dimensions={0}, use_global_device_ids=true | all-gather | bytes 20480 | tf_op jit(solution)/shard_map/all_gather | solution.py:134
  101.7 0.0 copy-done.8
  101.8 1.4 divide_convert_fusion
  103.2 0.0 all-gather.11.cloned.1.call-update
  103.2 29.5 %all-gather.9.cloned.1.call-done.e_ref = bf16[4096,768]{1,0:T(8,128)(2,1)} async-done(((bf16[512,768]{1,0:T(8,128)(2,1)}), bf16[4096,768]{1,0:T(8,128)(2,1)}) %all-gather.9.cloned.1.call-update) | async-done | bytes 6291472 | tf_op jit(solution)/shard_map/all_gather | solution.py:121
  132.8 0.0 copy-start.5
  132.8 2.8 copy-done.5
  135.5 0.0 copy-start.6
  135.5 2.8 copy-done.6
  138.3 72.2 %featurize.3.f_ref = bf16[4096,4096]{1,0:T(8,128)(2,1)} custom-call(bf16[4096,768]{1,0:T(8,128)(2,1)S(1)} %copy-done.6, bf16[768,4096]{1,0:T(8,128)(2,1)S(1)} %copy-done.5, f32[1,4096]{1,0:T(1,128)S(1)} %bitcast.24), custom_call_target="tpu_custom_call" | custom-call | flops 25769803776 | bytes 46137344 | tf_op jit(solution)/shard_map/featurize/pallas_call | solution.py:53
  210.6 0.0 all-gather.11.cloned.1.call-done
  210.6 12.0 %copy.11 = bf16[8192,512]{1,0:T(8,128)(2,1)} copy(bf16[8192,512]{0,1:T(8,128)(2,1)} %all-gather.11.cloned.1.call-done) | data formatting | bytes 16777216 | tf_op jit(solution)/shard_map/all_gather | solution.py:138
  222.5 4.5 %convert_reduce_fusion = f32[1024]{0:T(1024)S(1)} fusion(bf16[8,1024,512]{2,1,0:T(8,128)(2,1)} %bitcast.25), kind=kLoop, calls=%fused_computation | loop fusion | flops 8387584 | bytes 8392704 | tf_op jit(solution)/shard_map/reduce_sum | solution.py:140
  227.1 0.2 copy.12.m_ref
  227.3 0.0 copy-start.1
  227.3 46.2 %update.1 = f32[1024,4096]{1,0:T(8,128)} custom-call(bf16[8,1024,512]{2,1,0:T(8,128)(2,1)} %bitcast.26, bf16[4096,4096]{1,0:T(8,128)(2,1)} %featurize.3.f_ref, bf16[1024,4096]{1,0:T(8,128)(2,1)} %c_ref.1, f32[1024,1]{1,0:T(8,128)S(1)} %copy.12.m_ref), custom_call_target="tpu_custom_call" | custom-call | flops 34359738368 | bytes 67108864 | tf_op jit(solution)/shard_map/update/pallas_call | solution.py:92
  273.5 0.0 copy-done.1
  (3 shorter events, 0.1 us)
Async XLA Ops:
  6.5 1.0 copy-start
  6.5 30.2 %all-gather.7.cloned.1.call-start = ((), (), s32[]{:S(2)}) async-start(), calls=%async_computation.1 | async-start | bytes 1769472 | tf_op jit(solution)/shard_map/all_gather | solution.py:120
  8.2 28.5 %copy-start.7 = (f32[4096]{0:T(1024)S(1)}, f32[4096]{0:T(1024)}, u32[]{:S(2)}) copy-start(f32[4096]{0:T(1024)} %param.6) | copy-start | bytes 49156
  8.3 75.6 %reduce-scatter.2.cloned.1.call-start = ((), (), s32[]{:S(2)}) async-start(), calls=%async_computation.2 | async-start | bytes 6291456 | tf_op jit(solution)/shard_map/reduce_scatter | solution.py:129
  36.8 1.4 copy-start.2
  38.2 2.8 copy-start.4
  72.1 1.4 copy-start.3
  72.1 60.6 %all-gather.9.cloned.1.call-start = ((), (), s32[]{:S(2)}) async-start(), calls=%async_computation.3 | async-start | bytes 7077888 | tf_op jit(solution)/shard_map/all_gather | solution.py:121
  74.5 136.0 %all-gather.11.cloned.1.call-start = ((), (), s32[]{:S(2)}) async-start(), calls=%async_computation.4 | async-start | bytes 9437184 | tf_op jit(solution)/shard_map/all_gather | solution.py:138
  83.9 17.9 %copy-start.8 = (f32[1024,512]{0,1:T(8,128)S(1)}, f32[1024,512]{0,1:T(8,128)}, u32[]{:S(2)}) copy-start(f32[1024,512]{0,1:T(8,128)} %reduce-scatter.2.cloned.1.call-done) | copy-start | bytes 6291460
  132.8 2.8 copy-start.5
  135.5 2.8 copy-start.6
  227.3 46.2 %copy-start.1 = (bf16[256,768]{1,0:T(8,128)(2,1)S(1)}, bf16[256,768]{1,0:T(8,128)(2,1)}, u32[]{:S(2)}) copy-start(bf16[256,768]{1,0:T(8,128)(2,1)} %param.4) | copy-start | bytes 1179652
Sparse Core Ops, SparseCore 0:
  9.0 27.7 all-gather.6
  72.3 11.5 reduce-scatter.1
  85.9 46.8 all-gather.8
  134.7 54.3 all-gather.10

commit v2 on v1

v2 whole, which is shorter than its diff:
```python
import functools
import math

import jax
import jax.numpy as jnp
from jax import lax
from jax.experimental import pallas as pl
from jax.experimental.pallas import tpu as pltpu
from jax.sharding import PartitionSpec as P

F = 8192
SHARP_FACTOR = 1.5
PRIOR_MASS = 1.0

COS_COEFS = (
    1.4142135468471868,
    -0.7071066266011933,
    0.058925313538275806,
    -0.0019640317236862027,
    3.502984094725661e-05,
    -3.829489560381237e-07,
    2.4385896105334273e-09,
)
INV_TURN = 1.0 / (2.0 * math.pi)
TURN_COEFS = tuple(c * (2.0 * math.pi) ** (2 * k) for k, c in enumerate(COS_COEFS))


def scaled_cos(x):
    turns = x * INV_TURN
    r = turns - jnp.round(turns)
    u = r * r
    y = TURN_COEFS[-1]
    for c in TURN_COEFS[-2::-1]:
        y = y * u + c
    return y


def feature_kernel(sub_rows, sub_cols, e_ref, p_ref, b_ref, o_ref):
    rows, cols = o_ref.shape
    held = None
    for j in range(cols // sub_cols):
        cs = slice(j * sub_cols, (j + 1) * sub_cols)
        for i in range(rows // sub_rows):
            rs = slice(i * sub_rows, (i + 1) * sub_rows)
            x = jnp.dot(e_ref[rs, :], p_ref[:, cs], preferred_element_type=jnp.float32)
            if held is not None:
                hr, hc, hx = held
                o_ref[hr, hc] = scaled_cos(hx + b_ref[:, hc]).astype(jnp.bfloat16)
            held = rs, cs, x
    hr, hc, hx = held
    o_ref[hr, hc] = scaled_cos(hx + b_ref[:, hc]).astype(jnp.bfloat16)


def featurize(embeddings, projection, phases):
    rows, width = embeddings.shape
    cols = projection.shape[1]
    tr, tc = min(1024, rows), min(1024, cols)
    return pl.pallas_call(
        functools.partial(feature_kernel, min(128, tr), min(256, tc)),
        grid=(cols // tc, rows // tr),
        in_specs=[
            pl.BlockSpec((tr, width), lambda j, i: (i, 0)),
            pl.BlockSpec((width, tc), lambda j, i: (0, j)),
            pl.BlockSpec((1, tc), lambda j, i: (0, j)),
        ],
        out_specs=pl.BlockSpec((tr, tc), lambda j, i: (i, j)),
        out_shape=jax.ShapeDtypeStruct((rows, cols), jnp.bfloat16),
        compiler_params=pltpu.CompilerParams(vmem_limit_bytes=32 << 20),
        cost_estimate=pl.CostEstimate(
            flops=6 * rows * width * cols,
            bytes_accessed=2 * (rows * cols + rows * width + width * cols),
            transcendentals=0,
        ),
        name="featurize",
    )(embeddings, projection, phases.reshape(1, cols))


def score_kernel(tile, c_ref, f_ref, s_ref, o_ref):
    cents = c_ref.shape[0]
    for i in range(cents // tile):
        rs = slice(i * tile, (i + 1) * tile)
        inner = lax.dot_general(
            c_ref[rs, :],
            f_ref[...],
            (((1,), (1,)), ((), ())),
            preferred_element_type=jnp.float32,
        )
        o_ref[0, rs, :] = 2.0 * inner - s_ref[rs, :]


def score(centroids, features, center_sq, groups):
    cents, cols = centroids.shape
    rows = features.shape[0]
    size = rows // groups
    return pl.pallas_call(
        functools.partial(score_kernel, min(256, cents)),
        grid=(groups,),
        in_specs=[
            pl.BlockSpec((cents, cols), lambda g: (0, 0)),
            pl.BlockSpec((size, cols), lambda g: (g, 0)),
            pl.BlockSpec((cents, 1), lambda g: (0, 0)),
        ],
        out_specs=pl.BlockSpec((1, cents, size), lambda g: (g, 0, 0)),
        out_shape=jax.ShapeDtypeStruct((groups, cents, size), jnp.float32),
        compiler_params=pltpu.CompilerParams(vmem_limit_bytes=40 << 20),
        cost_estimate=pl.CostEstimate(
            flops=2 * rows * cents * cols,
            bytes_accessed=2 * (rows * cols + cents * cols) + 4 * rows * cents,
            transcendentals=0,
        ),
        name="score",
    )(centroids, features, center_sq)


def update_kernel(n_data, n_feat, i_ref, r_ref, c_ref, *refs):
    f_refs, (o_ref, k_ref, m_ref) = refs[:n_data], refs[n_data:]
    size = r_ref.shape[2]

    @pl.when(pl.program_id(0) == 0)
    def _():
        mass = jnp.zeros(m_ref.shape, jnp.float32)
        for g in range(n_data * n_feat):
            part = r_ref[i_ref[g]]
            k_ref[:, g * size : (g + 1) * size] = part
            mass += jnp.sum(part.astype(jnp.float32), axis=1, keepdims=True)
        m_ref[...] = mass

    total = PRIOR_MASS * c_ref[...].astype(jnp.float32)
    depth = n_feat * size
    for s in range(n_data):
        total += jnp.dot(
            k_ref[:, s * depth : (s + 1) * depth],
            f_refs[s][...],
            preferred_element_type=jnp.float32,
        )
    o_ref[...] = total / (m_ref[...] + PRIOR_MASS)


def update(order, resp, centroids, features, n_feat):
    groups, cents, size = resp.shape
    n_data = len(features)
    depth, cols = features[0].shape
    rows = n_data * depth
    tc = min(512, cols)
    return pl.pallas_call(
        functools.partial(update_kernel, n_data, n_feat),
        grid=(cols // tc,),
        in_specs=[
            pl.BlockSpec(memory_space=pltpu.SMEM),
            pl.BlockSpec(
                (groups, cents, size), lambda j: (0, 0, 0), pipeline_mode=pl.Buffered(1)
            ),
            pl.BlockSpec((cents, tc), lambda j: (0, j)),
        ]
        + [pl.BlockSpec((depth, tc), lambda j: (0, j))] * n_data,
        out_specs=pl.BlockSpec((cents, tc), lambda j: (0, j)),
        out_shape=jax.ShapeDtypeStruct((cents, cols), jnp.float32),
        scratch_shapes=[
            pltpu.VMEM((cents, rows), jnp.bfloat16),
            pltpu.VMEM((cents, 1), jnp.float32),
        ],
        compiler_params=pltpu.CompilerParams(vmem_limit_bytes=52 << 20),
        cost_estimate=pl.CostEstimate(
            flops=2 * rows * cents * cols,
            bytes_accessed=2 * (rows * cols + rows * cents) + 6 * cents * cols,
            transcendentals=0,
        ),
        name="update",
    )(order, resp, centroids, *features)


def my_part(x, axis_name):
    size = x.shape[0] // lax.axis_size(axis_name)
    return lax.dynamic_slice_in_dim(x, lax.axis_index(axis_name) * size, size, 0)


def from_others(x, axis_name):
    n = lax.axis_size(axis_name)
    return [
        lax.ppermute(x, axis_name, [(i, (i + s) % n) for i in range(n)]) for s in range(1, n)
    ]


def shards(embeddings, projection, phases, centroids):
    sharpness = SHARP_FACTOR / math.sqrt(F)
    n_data, n_feat = lax.axis_size("dp"), lax.axis_size("feat")
    dp, feat = lax.axis_index("dp"), lax.axis_index("feat")
    own = lax.all_gather(my_part(embeddings, "feat"), ("cent", "feat"), axis=0, tiled=True)
    halves = from_others(my_part(own, "feat"), "dp")
    wide = centroids.astype(jnp.float32)
    center_sq = jnp.sum(wide * wide, axis=1, keepdims=True)
    own_features = featurize(own, projection, phases)
    partial_value = score(centroids, own_features, center_sq, n_feat)
    partial_value, *halves = lax.optimization_barrier((partial_value, *halves))
    others = [
        jnp.concatenate([half] + from_others(half, "feat"), axis=0) for half in halves
    ]
    whole_value = lax.psum_scatter(partial_value, "feat", scatter_dimension=0)
    whole_value, *others = lax.optimization_barrier((whole_value, *others))
    logits = sharpness * whole_value
    top = jnp.max(logits, axis=0)
    local_sum = jnp.sum(jnp.exp(logits - top[None, :]), axis=0)
    stats = jnp.stack([top, local_sum])
    stats = jnp.stack([stats] + from_others(stats, "cent"))
    peak = jnp.max(stats[:, 0], axis=0)
    norm = jnp.sum(stats[:, 1] * jnp.exp(stats[:, 0] - peak[None, :]), axis=0)
    resp = (jnp.exp(logits - peak[None, :]) / norm[None, :]).astype(jnp.bfloat16)
    all_resp = lax.all_gather(resp, ("dp", "feat"), axis=0, tiled=False)
    features = [own_features] + [featurize(x, projection, phases) for x in others]
    order = [dp * n_feat + t for t in range(n_feat)] + [
        (dp + n_data - s) % n_data * n_feat + (feat + n_feat - t) % n_feat
        for s in range(1, n_data)
        for t in range(n_feat)
    ]
    order = jnp.stack(order).astype(jnp.int32)
    return update(order, all_resp, centroids, features, n_feat)


def solution(mesh):
    return jax.shard_map(
        shards,
        mesh=mesh,
        in_specs=(P(("dp", "cent"), None), P(None, "feat"), P("feat"), P("cent", "feat")),
        out_specs=P("cent", "feat"),
        check_vma=False,
    )
```

time: 281 us -> 213 us (0.76)
  waiting for transfers between devices: 62.3 us -> 30.7 us
  Pallas kernels: 137 us -> 118 us
  blocking collectives: 13.7 us -> 0 us
  matrix products: 12.6 us -> 0 us
  starting transfers between devices: 0.13 us -> 11 us
    all_gather x1 -> x0, waiting for transfers between devices: 29.5 us -> none  [shards(): lax.all_gather(my_part(own, 'feat'), ('dp', 'feat'), axis=0, tiled=True)]
    pallas_call x3 -> x6, Pallas kernels: 137 us -> 118 us  [the longest x4 62.2 us: featurize(): pl.pallas_call(functools.partial(feature_kernel, min(128, tr), min(256, t...]
    all_gather x1 -> x0, blocking collectives: 13.7 us -> none  [shards(): lax.all_gather(jnp.stack([top, local_sum]), 'cent', axis=0, tiled=False)]
    dot_general x1 -> x0, matrix products: 12.6 us -> none  [shards(): lax.dot_general(centroids, own_features, (((1,), (1,)), ((), ())), prefer...]
    all_gather x1 -> x0, local copies, waits for them, and re-layouts: 12 us -> none  [shards(): all_resp = lax.all_gather(resp, ('dp', 'feat'), axis=0, tiled=False)]
    unnamed x18 -> x30, local copies, waits for them, and re-layouts: 12.1 us -> 23.1 us
    ppermute x0 -> x9, starting transfers between devices: none -> 10.9 us  [from_others(): lax.ppermute(x, axis_name, [(i, (i + s) % n) for i in range(n)])]
    reduce_scatter x1, waiting for transfers between devices: 9.28 us -> 4.02 us  [shards(): whole_value = lax.psum_scatter(partial_value, 'feat', scatter_dimension=0)]
  transfers between devices with their start and end apart: 4 -> 12, of which waited for: 3 -> 4; matrix products, arithmetic and copies ran while one was open for 4% -> 5% of each run, Pallas kernels for 26% -> 35%
where the time goes in v2:
time: 213 us
  Pallas kernels  118 us (55%)
  waiting for transfers between devices  30.7 us (14%)
  local copies, waits for them, and re-layouts  25.5 us (12%)
  other arithmetic  14 us (7%)
  between operations  13.3 us (6%)
  starting transfers between devices  11 us (5%)
    pallas_call x4, Pallas kernels, featurize(): pl.pallas_call(functools.partial(feature_kernel, min(128, tr), min(256, t...  62.2 us
    pallas_call x1, Pallas kernels, update(): pl.pallas_call(functools.partial(update_kernel, n_data, n_feat), grid=(co...  44.7 us
    all_gather x1, waiting for transfers between devices, shards(): lax.all_gather(my_part(embeddings, 'feat'), ('cent', 'feat'), axis=0, til...  23.2 us
    unnamed x30, local copies, waits for them, and re-layouts  23.1 us
    pallas_call x1, Pallas kernels, score(): pl.pallas_call(functools.partial(score_kernel, min(256, cents)), grid=(gr...  11.3 us
    ppermute x9, starting transfers between devices, from_others(): lax.ppermute(x, axis_name, [(i, (i + s) % n) for i in range(n)])  10.9 us
    reduce_sum x1, other arithmetic, shards(): center_sq = jnp.sum(wide * wide, axis=1, keepdims=True)  5.07 us
    concatenate x3, other arithmetic, shards(): jnp.concatenate([half] + from_others(half, 'feat'), axis=0)  5.06 us
  transfers between devices with their start and end apart: 12, of which 4 were waited for; matrix products, arithmetic and copies ran while one was open for 5% of the time, Pallas kernels for 35%

profile of v2, /device:TPU:0, one launch (start us, length us, event | category | flops | bytes accessed | tf_op | source)
XLA Modules:
  0.0 212.7 jit_solution(5864774682940801180)
XLA Ops:
  6.5 1.0 copy-done
  7.5 0.7 constant_dynamic-slice_fusion.1
  8.2 0.0 all-gather.4.cloned.1.call-update
  8.2 0.0 reduce-scatter.2.cloned.1.call-start
  8.3 5.1 %multiply_reduce_fusion = f32[1024]{0:T(1024)S(1)} fusion(bf16[1024,4096]{1,0:T(8,128)(2,1)} %c_ref.3), kind=kLoop, calls=%fused_computation | loop fusion | flops 12581888 | bytes 8392704 | tf_op jit(solution)/shard_map/reduce_sum | solution.py:191
  13.4 0.2 copy.8.s_ref
  13.6 23.2 %all-gather.4.cloned.1.call-done.e_ref = bf16[1024,768]{1,0:T(8,128)(2,1)} async-done(((bf16[128,768]{1,0:T(8,128)(2,1)}), bf16[1024,768]{1,0:T(8,128)(2,1)}) %all-gather.4.cloned.1.call-update) | async-done | bytes 1572880 | tf_op jit(solution)/shard_map/all_gather | solution.py:188
  36.8 1.3 constant_dynamic-slice_fusion
  38.1 2.4 %collective-permute-start.2 = (bf16[512,768]{1,0:T(8,128)(2,1)S(1)}, bf16[512,768]{1,0:T(8,128)(2,1)}, u32[]{:S(2)}, u32[]{:S(2)}) collective-permute-start(bf16[512,768]{1,0:T(8,128)(2,1)S(1)} %constant_dynamic-slice_fusion), channel_id=1, source_target_pairs={{0,24},{8,0},{16,8},{24,16},{1,25},{9,1},{17,9},{25,17},{2,26},{10... | collective-permute-start | bytes 2359304 | tf_op jit(solution)/shard_map/ppermute | solution.py:180
  40.6 0.6 collective-permute-start.1
  41.1 0.6 collective-permute-start
  41.7 1.4 copy-done.4
  43.1 2.8 %copy-done.5 = bf16[768,4096]{1,0:T(8,128)(2,1)S(1)} copy-done((bf16[768,4096]{1,0:T(8,128)(2,1)S(1)}, bf16[768,4096]{1,0:T(8,128)(2,1)}, u32[]{:S(2)}) %copy-start.5) | copy-done | bytes 6291480
  45.9 15.6 %featurize.4.f_ref.refs_0_ = bf16[1024,4096]{1,0:T(8,128)(2,1)S(1)} custom-call(bf16[1024,768]{1,0:T(8,128)(2,1)S(1)} %copy-done.4, bf16[768,4096]{1,0:T(8,128)(2,1)S(1)} %copy-done.5, f32[1,4096]{1,0:T(1,128)S(1)} %bitcast.32), custom_call_target="tpu_custom_call" | custom-call | flops 19327352832 | bytes 16252928 | tf_op jit(solution)/shard_map/featurize/pallas_call | solution.py:58
  61.4 3.2 %copy-done.8 = bf16[1024,4096]{1,0:T(8,128)(2,1)} copy-done((bf16[1024,4096]{1,0:T(8,128)(2,1)}, bf16[1024,4096]{1,0:T(8,128)(2,1)S(1)}, u32[]{:S(2)}) %copy-start.8) | copy-done | bytes 8388632
  64.7 11.3 %score.1 = f32[2,1024,512]{2,1,0:T(8,128)S(1)} custom-call(bf16[1024,4096]{1,0:T(8,128)(2,1)S(1)} %bitcast.31, bf16[1024,4096]{1,0:T(8,128)(2,1)} %copy-done.8, f32[1024,1]{1,0:T(8,128)S(1)} %copy.8.s_ref), custom_call_target="tpu_custom_call" | custom-call | flops 8589934592 | bytes 20971520 | tf_op jit(solution)/shard_map/score/pallas_call | solution.py:95
  75.9 0.0 copy-start.2
  76.0 2.0 copy-done.2
  78.0 0.0 collective-permute-done
  78.0 0.0 reduce-scatter.2.cloned.1.call-update
  78.0 0.0 all-gather.6.cloned.1.call-start
  78.0 0.1 collective-permute-start.3
  78.1 0.5 collective-permute-start.4
  78.6 0.1 collective-permute-start.5
  78.7 1.9 collective-permute-done.3
  80.6 1.2 pad_maximum_fusion.e_ref
  81.9 1.2 pad_maximum_fusion.1.e_ref
  83.1 2.6 %pad_maximum_fusion.2.e_ref = bf16[1024,768]{1,0:T(8,128)(2,1)} fusion(bf16[512,768]{1,0:T(8,128)(2,1)S(1)} %collective-permute-done.5, bf16[512,768]{1,0:T(8,128)(2,1)} %collective-permute-done.2), kind=kLoop, calls=%fused_computation.6 | loop fusion | flops 3145728 | bytes 3145728 | tf_op jit(solution)/shard_map/concatenate | solution.py:196
  85.7 4.0 %reduce-scatter.2.cloned.1.call-done = f32[1,1024,512]{2,1,0:T(8,128)} async-done(((f32[2,1024,512]{2,1,0:T(8,128)}), f32[1,1024,512]{2,1,0:T(8,128)}) %reduce-scatter.2.cloned.1.call-update) | async-done | bytes 2097168 | tf_op jit(solution)/shard_map/reduce_scatter | solution.py:198
  89.7 2.0 multiply_reduce_fusion.1
  91.7 0.2 copy-done.12
  91.9 0.4 exponential_reduce_fusion
  92.4 2.9 %collective-permute-start.7 = (f32[2,512]{1,0:T(2,128)S(1)}, f32[2,512]{1,0:T(2,128)S(1)}, u32[]{:S(2)}, u32[]{:S(2)}) collective-permute-start(f32[2,512]{1,0:T(2,128)S(1)} %get-tuple-element.22), channel_id=1, source_target_pairs={{0,2},{1,3},{2,0},{3,1},{4,6},{5,7},{6,4},{7,5},{8,10},{9,11},{10,... | collective-permute-start | bytes 12296 | tf_op jit(solution)/shard_map/ppermute | solution.py:180
  95.2 1.5 collective-permute-start.6
  96.7 2.3 %collective-permute-start.8 = (f32[2,512]{1,0:T(2,128)S(1)}, f32[2,512]{1,0:T(2,128)S(1)}, u32[]{:S(2)}, u32[]{:S(2)}) collective-permute-start(f32[2,512]{1,0:T(2,128)S(1)} %get-tuple-element.22), channel_id=1, source_target_pairs={{0,3},{1,0},{2,1},{3,2},{4,7},{5,4},{6,5},{7,6},{8,11},{9,8},{10,9... | collective-permute-start | bytes 12296 | tf_op jit(solution)/shard_map/ppermute | solution.py:180
  99.1 0.0 collective-permute-done.7
  99.1 1.6 collective-permute-done.6
  100.7 1.4 divide_convert_fusion
  102.1 0.0 all-gather.6.cloned.1.call-update
  102.2 0.1 stack.59.i_ref
  102.3 2.8 %copy-done.6 = bf16[768,4096]{1,0:T(8,128)(2,1)S(1)} copy-done((bf16[768,4096]{1,0:T(8,128)(2,1)S(1)}, bf16[768,4096]{1,0:T(8,128)(2,1)}, u32[]{:S(2)}) %copy-start.6) | copy-done | bytes 6291480
  105.1 15.5 %featurize.5.refs_1_ = bf16[1024,4096]{1,0:T(8,128)(2,1)S(1)} custom-call(bf16[1024,768]{1,0:T(8,128)(2,1)S(1)} %pad_maximum_fusion.e_ref, bf16[768,4096]{1,0:T(8,128)(2,1)S(1)} %copy-done.6, f32[1,4096]{1,0:T(1,128)S(1)} %bitcast.33), custom_call_target="tpu_custom_call" | custom-call | flops 19327352832 | bytes 16252928 | tf_op jit(solution)/shard_map/featurize/pallas_call | solution.py:58
  120.6 3.2 %copy-done.9 = bf16[1024,4096]{1,0:T(8,128)(2,1)} copy-done((bf16[1024,4096]{1,0:T(8,128)(2,1)}, bf16[1024,4096]{1,0:T(8,128)(2,1)S(1)}, u32[]{:S(2)}) %copy-start.9) | copy-done | bytes 8388632
  123.8 15.5 %featurize.6.refs_2_ = bf16[1024,4096]{1,0:T(8,128)(2,1)S(1)} custom-call(bf16[1024,768]{1,0:T(8,128)(2,1)S(1)} %pad_maximum_fusion.1.e_ref, bf16[768,4096]{1,0:T(8,128)(2,1)S(1)} %copy-done.6, f32[1,4096]{1,0:T(1,128)S(1)} %bitcast.34), custom_call_target="tpu_custom_call" | custom-call | flops 19327352832 | bytes 16252928 | tf_op jit(solution)/shard_map/featurize/pallas_call | solution.py:58
  139.4 3.2 %copy-done.10 = bf16[1024,4096]{1,0:T(8,128)(2,1)} copy-done((bf16[1024,4096]{1,0:T(8,128)(2,1)}, bf16[1024,4096]{1,0:T(8,128)(2,1)S(1)}, u32[]{:S(2)}) %copy-start.10) | copy-done | bytes 8388632
  142.6 15.6 %featurize.7.refs_3_ = bf16[1024,4096]{1,0:T(8,128)(2,1)S(1)} custom-call(bf16[1024,768]{1,0:T(8,128)(2,1)S(1)} %copy-done.3, bf16[768,4096]{1,0:T(8,128)(2,1)S(1)} %copy-done.6, f32[1,4096]{1,0:T(1,128)S(1)} %bitcast.35), custom_call_target="tpu_custom_call" | custom-call | flops 19327352832 | bytes 16252928 | tf_op jit(solution)/shard_map/featurize/pallas_call | solution.py:58
  158.2 3.2 %copy-done.11 = bf16[1024,4096]{1,0:T(8,128)(2,1)} copy-done((bf16[1024,4096]{1,0:T(8,128)(2,1)}, bf16[1024,4096]{1,0:T(8,128)(2,1)S(1)}, u32[]{:S(2)}) %copy-start.11) | copy-done | bytes 8388632
  161.4 44.7 %update.1 = f32[1024,4096]{1,0:T(8,128)} custom-call(s32[8]{0:T(128)S(1)} %stack.59.i_ref, bf16[8,1024,512]{2,1,0:T(8,128)(2,1)} %bitcast.44, bf16[1024,4096]{1,0:T(8,128)(2,1)} %c_ref.3, bf16[1024,4096]{1,0:T(8,128)(2,1)} %copy-done.8, bf16[1024,4096]{1,0:T(8,128)(2,1)} %copy-done.9, bf16[1024,4096]{1,0:T(8,128)(2,1)} %copy-done.10, ...), custom_call_target="tpu_custom_call" | custom-call | flops 34359738368 | bytes 67108864 | tf_op jit(solution)/shard_map/update/pallas_call | solution.py:145
  (35 shorter events, 0.2 us)
Async XLA Ops:
  6.5 1.0 copy-start
  6.5 30.2 %all-gather.4.cloned.1.call-start = ((), (), s32[]{:S(2)}) async-start(), calls=%async_computation.1 | async-start | bytes 1769472 | tf_op jit(solution)/shard_map/all_gather | solution.py:188
  8.2 81.5 %reduce-scatter.2.cloned.1.call-start = ((), (), s32[]{:S(2)}) async-start(), calls=%async_computation.2 | async-start | bytes 6291456 | tf_op jit(solution)/shard_map/reduce_scatter | solution.py:198
  13.4 28.3 %copy-start.7 = (f32[4096]{0:T(1024)S(1)}, f32[4096]{0:T(1024)}, u32[]{:S(2)}) copy-start(f32[4096]{0:T(1024)} %param.6) | copy-start | bytes 49156
  36.8 27.9 %slice-start = ((s8[8388608]{0:T(1024)(128)(4,1)}), s8[4194304]{0:T(1024)(128)(4,1)S(1)}, s32[]{:S(2)}) async-start(s8[8388608]{0:T(1024)(128)(4,1)} %bitcast.30), calls=%async_computation.4 | async-start | bytes 8388608
  38.1 39.8 %collective-permute-start.2 = (bf16[512,768]{1,0:T(8,128)(2,1)S(1)}, bf16[512,768]{1,0:T(8,128)(2,1)}, u32[]{:S(2)}, u32[]{:S(2)}) collective-permute-start(bf16[512,768]{1,0:T(8,128)(2,1)S(1)} %constant_dynamic-slice_fusion), channel_id=1, source_target_pairs={{0,24},{8,0},{16,8},{24,16},{1,25},{9,1},{17,9},{25,17},{2,26},{10... | collective-permute-start | bytes 2359304 | tf_op jit(solution)/shard_map/ppermute | solution.py:180
  40.6 37.4 %collective-permute-start.1 = (bf16[512,768]{1,0:T(8,128)(2,1)S(1)}, bf16[512,768]{1,0:T(8,128)(2,1)}, u32[]{:S(2)}, u32[]{:S(2)}) collective-permute-start(bf16[512,768]{1,0:T(8,128)(2,1)S(1)} %constant_dynamic-slice_fusion), channel_id=1, source_target_pairs={{0,16},{8,24},{16,0},{24,8},{1,17},{9,25},{17,1},{25,9},{2,18},{10... | collective-permute-start | bytes 2359304 | tf_op jit(solution)/shard_map/ppermute | solution.py:180
  41.1 36.9 %collective-permute-start = (bf16[512,768]{1,0:T(8,128)(2,1)S(1)}, bf16[512,768]{1,0:T(8,128)(2,1)}, u32[]{:S(2)}, u32[]{:S(2)}) collective-permute-start(bf16[512,768]{1,0:T(8,128)(2,1)S(1)} %constant_dynamic-slice_fusion), channel_id=1, source_target_pairs={{0,8},{8,16},{16,24},{24,0},{1,9},{9,17},{17,25},{25,1},{2,10},{10... | collective-permute-start | bytes 2359304 | tf_op jit(solution)/shard_map/ppermute | solution.py:180
  41.7 1.4 copy-start.4
  43.1 2.8 %copy-start.5 = (bf16[768,4096]{1,0:T(8,128)(2,1)S(1)}, bf16[768,4096]{1,0:T(8,128)(2,1)}, u32[]{:S(2)}) copy-start(bf16[768,4096]{1,0:T(8,128)(2,1)} %p_ref.7) | copy-start | bytes 18874372
  45.9 18.8 %slice-start.1 = ((s8[8388608]{0:T(1024)(128)(4,1)}), s8[4194304]{0:T(1024)(128)(4,1)S(1)}, s32[]{:S(2)}) async-start(s8[8388608]{0:T(1024)(128)(4,1)} %bitcast.30), calls=%async_computation.5 | async-start | bytes 8388608
  61.4 3.2 %copy-start.8 = (bf16[1024,4096]{1,0:T(8,128)(2,1)}, bf16[1024,4096]{1,0:T(8,128)(2,1)S(1)}, u32[]{:S(2)}) copy-start(bf16[1024,4096]{1,0:T(8,128)(2,1)S(1)} %featurize.4.f_ref.refs_0_) | copy-start | bytes 25165828
  75.9 2.0 copy-start.2
  78.0 83.4 %all-gather.6.cloned.1.call-start = ((), (), s32[]{:S(2)}) async-start(), calls=%async_computation.3 | async-start | bytes 9437184 | tf_op jit(solution)/shard_map/all_gather | solution.py:208
  78.0 2.6 %collective-permute-start.3 = (bf16[512,768]{1,0:T(8,128)(2,1)}, bf16[512,768]{1,0:T(8,128)(2,1)S(1)}, u32[]{:S(2)}, u32[]{:S(2)}) collective-permute-start(bf16[512,768]{1,0:T(8,128)(2,1)} %collective-permute-done), channel_id=1, source_target_pairs={{0,4},{4,0},{1,5},{5,1},{2,6},{6,2},{3,7},{7,3},{8,12},{12,8},{9,1... | collective-permute-start | bytes 2359304 | tf_op jit(solution)/shard_map/ppermute | solution.py:180
  78.1 3.7 %collective-permute-start.4 = (bf16[512,768]{1,0:T(8,128)(2,1)}, bf16[512,768]{1,0:T(8,128)(2,1)S(1)}, u32[]{:S(2)}, u32[]{:S(2)}) collective-permute-start(bf16[512,768]{1,0:T(8,128)(2,1)} %collective-permute-done.1), channel_id=1, source_target_pairs={{0,4},{4,0},{1,5},{5,1},{2,6},{6,2},{3,7},{7,3},{8,12},{12,8},{9,1... | collective-permute-start | bytes 2359304 | tf_op jit(solution)/shard_map/ppermute | solution.py:180
  78.6 4.5 %collective-permute-start.5 = (bf16[512,768]{1,0:T(8,128)(2,1)}, bf16[512,768]{1,0:T(8,128)(2,1)S(1)}, u32[]{:S(2)}, u32[]{:S(2)}) collective-permute-start(bf16[512,768]{1,0:T(8,128)(2,1)} %collective-permute-done.2), channel_id=1, source_target_pairs={{0,4},{4,0},{1,5},{5,1},{2,6},{6,2},{3,7},{7,3},{8,12},{12,8},{9,1... | collective-permute-start | bytes 2359304 | tf_op jit(solution)/shard_map/ppermute | solution.py:180
  89.7 2.2 %copy-start.12 = (f32[1,1024,512]{2,1,0:T(8,128)S(1)}, f32[1,1024,512]{2,1,0:T(8,128)}, u32[]{:S(2)}) copy-start(f32[1,1024,512]{2,1,0:T(8,128)} %reduce-scatter.2.cloned.1.call-done) | copy-start | bytes 6291460
  92.4 6.7 %collective-permute-start.7 = (f32[2,512]{1,0:T(2,128)S(1)}, f32[2,512]{1,0:T(2,128)S(1)}, u32[]{:S(2)}, u32[]{:S(2)}) collective-permute-start(f32[2,512]{1,0:T(2,128)S(1)} %get-tuple-element.22), channel_id=1, source_target_pairs={{0,2},{1,3},{2,0},{3,1},{4,6},{5,7},{6,4},{7,5},{8,10},{9,11},{10,... | collective-permute-start | bytes 12296 | tf_op jit(solution)/shard_map/ppermute | solution.py:180
  95.2 5.4 %collective-permute-start.6 = (f32[2,512]{1,0:T(2,128)S(1)}, f32[2,512]{1,0:T(2,128)S(1)}, u32[]{:S(2)}, u32[]{:S(2)}) collective-permute-start(f32[2,512]{1,0:T(2,128)S(1)} %get-tuple-element.22), channel_id=1, source_target_pairs={{0,1},{1,2},{2,3},{3,0},{4,5},{5,6},{6,7},{7,4},{8,9},{9,10},{10,1... | collective-permute-start | bytes 12296 | tf_op jit(solution)/shard_map/ppermute | solution.py:180
  96.7 3.9 %collective-permute-start.8 = (f32[2,512]{1,0:T(2,128)S(1)}, f32[2,512]{1,0:T(2,128)S(1)}, u32[]{:S(2)}, u32[]{:S(2)}) collective-permute-start(f32[2,512]{1,0:T(2,128)S(1)} %get-tuple-element.22), channel_id=1, source_target_pairs={{0,3},{1,0},{2,1},{3,2},{4,7},{5,4},{6,5},{7,6},{8,11},{9,8},{10,9... | collective-permute-start | bytes 12296 | tf_op jit(solution)/shard_map/ppermute | solution.py:180
  102.3 2.8 %copy-start.6 = (bf16[768,4096]{1,0:T(8,128)(2,1)S(1)}, bf16[768,4096]{1,0:T(8,128)(2,1)}, u32[]{:S(2)}) copy-start(bf16[768,4096]{1,0:T(8,128)(2,1)} %p_ref.7) | copy-start | bytes 18874372
  120.6 3.2 %copy-start.9 = (bf16[1024,4096]{1,0:T(8,128)(2,1)}, bf16[1024,4096]{1,0:T(8,128)(2,1)S(1)}, u32[]{:S(2)}) copy-start(bf16[1024,4096]{1,0:T(8,128)(2,1)S(1)} %featurize.5.refs_1_) | copy-start | bytes 25165828
  123.8 18.8 %copy-start.3 = (bf16[1024,768]{1,0:T(8,128)(2,1)S(1)}, bf16[1024,768]{1,0:T(8,128)(2,1)}, u32[]{:S(2)}) copy-start(bf16[1024,768]{1,0:T(8,128)(2,1)} %pad_maximum_fusion.2.e_ref) | copy-start | bytes 4718596
  139.4 3.2 %copy-start.10 = (bf16[1024,4096]{1,0:T(8,128)(2,1)}, bf16[1024,4096]{1,0:T(8,128)(2,1)S(1)}, u32[]{:S(2)}) copy-start(bf16[1024,4096]{1,0:T(8,128)(2,1)S(1)} %featurize.6.refs_2_) | copy-start | bytes 25165828
  158.2 3.2 %copy-start.11 = (bf16[1024,4096]{1,0:T(8,128)(2,1)}, bf16[1024,4096]{1,0:T(8,128)(2,1)S(1)}, u32[]{:S(2)}) copy-start(bf16[1024,4096]{1,0:T(8,128)(2,1)S(1)} %featurize.7.refs_3_) | copy-start | bytes 25165828
  161.4 44.7 %copy-start.1 = (bf16[256,768]{1,0:T(8,128)(2,1)S(1)}, bf16[256,768]{1,0:T(8,128)(2,1)}, u32[]{:S(2)}) copy-start(bf16[256,768]{1,0:T(8,128)(2,1)} %param.4) | copy-start | bytes 1179652
Sparse Core Ops, SparseCore 0:
  9.0 27.7 all-gather.3
  78.1 11.5 reduce-scatter.1
  102.2 55.7 all-gather.5

commit v3 on v2

--- a/solution.py
+++ b/solution.py
@@ -51,28 +51,38 @@
     o_ref[hr, hc] = scaled_cos(hx + b_ref[:, hc]).astype(jnp.bfloat16)
 
 
-def featurize(embeddings, projection, phases):
+def featurize(embeddings, projection, phases, total_rows, first_row, held):
     rows, width = embeddings.shape
     cols = projection.shape[1]
     tr, tc = min(1024, rows), min(1024, cols)
+    first = first_row // tr
+    kernel = functools.partial(feature_kernel, min(128, tr), min(256, tc))
+    in_specs = [
+        pl.BlockSpec((tr, width), lambda j, i: (i, 0)),
+        pl.BlockSpec((width, tc), lambda j, i: (0, j)),
+        pl.BlockSpec((1, tc), lambda j, i: (0, j)),
+    ]
+    operands = [embeddings, projection, phases.reshape(1, cols)]
+    aliases = {}
+    if held is not None:
+        in_specs.append(pl.BlockSpec(memory_space=pl.ANY))
+        operands.append(held)
+        aliases = {3: 0}
     return pl.pallas_call(
-        functools.partial(feature_kernel, min(128, tr), min(256, tc)),
+        lambda *refs: kernel(*refs[:3], refs[-1]),
         grid=(cols // tc, rows // tr),
-        in_specs=[
-            pl.BlockSpec((tr, width), lambda j, i: (i, 0)),
-            pl.BlockSpec((width, tc), lambda j, i: (0, j)),
-            pl.BlockSpec((1, tc), lambda j, i: (0, j)),
-        ],
-        out_specs=pl.BlockSpec((tr, tc), lambda j, i: (i, j)),
-        out_shape=jax.ShapeDtypeStruct((rows, cols), jnp.bfloat16),
-        compiler_params=pltpu.CompilerParams(vmem_limit_bytes=32 << 20),
+        in_specs=in_specs,
+        out_specs=pl.BlockSpec((tr, tc), lambda j, i: (first + i, j)),
+        out_shape=jax.ShapeDtypeStruct((total_rows, cols), jnp.bfloat16),
+        input_output_aliases=aliases,
+        compiler_params=pltpu.CompilerParams(vmem_limit_bytes=44 << 20),
         cost_estimate=pl.CostEstimate(
             flops=6 * rows * width * cols,
             bytes_accessed=2 * (rows * cols + rows * width + width * cols),
             transcendentals=0,
         ),
         name="featurize",
-    )(embeddings, projection, phases.reshape(1, cols))
+    )(*operands)
 
 
 def score_kernel(tile, c_ref, f_ref, s_ref, o_ref):
@@ -88,9 +98,8 @@
         o_ref[0, rs, :] = 2.0 * inner - s_ref[rs, :]
 
 
-def score(centroids, features, center_sq, groups):
+def score(centroids, features, center_sq, rows, groups):
     cents, cols = centroids.shape
-    rows = features.shape[0]
     size = rows // groups
     return pl.pallas_call(
         functools.partial(score_kernel, min(256, cents)),
@@ -112,47 +121,42 @@
     )(centroids, features, center_sq)
 
 
-def update_kernel(n_data, n_feat, i_ref, r_ref, c_ref, *refs):
-    f_refs, (o_ref, k_ref, m_ref) = refs[:n_data], refs[n_data:]
-    size = r_ref.shape[2]
+def update_kernel(n_parts, i_ref, *refs):
+    r_refs = refs[:n_parts]
+    c_ref, f_ref, o_ref, k_ref, m_ref = refs[n_parts:]
+    size = r_refs[0].shape[1]
 
     @pl.when(pl.program_id(0) == 0)
     def _():
         mass = jnp.zeros(m_ref.shape, jnp.float32)
-        for g in range(n_data * n_feat):
-            part = r_ref[i_ref[g]]
-            k_ref[:, g * size : (g + 1) * size] = part
+        for g in range(n_parts):
+            part = r_refs[g][...]
+            k_ref[:, pl.ds(pl.multiple_of(i_ref[g] * size, size), size)] = part
             mass += jnp.sum(part.astype(jnp.float32), axis=1, keepdims=True)
         m_ref[...] = mass
 
-    total = PRIOR_MASS * c_ref[...].astype(jnp.float32)
-    depth = n_feat * size
-    for s in range(n_data):
-        total += jnp.dot(
-            k_ref[:, s * depth : (s + 1) * depth],
-            f_refs[s][...],
-            preferred_element_type=jnp.float32,
-        )
-    o_ref[...] = total / (m_ref[...] + PRIOR_MASS)
-
-
-def update(order, resp, centroids, features, n_feat):
-    groups, cents, size = resp.shape
-    n_data = len(features)
-    depth, cols = features[0].shape
-    rows = n_data * depth
+    total = jnp.dot(k_ref[...], f_ref[...], preferred_element_type=jnp.float32)
+    o_ref[...] = (total + PRIOR_MASS * c_ref[...].astype(jnp.float32)) / (
+        m_ref[...] + PRIOR_MASS
+    )
+
+
+def update(places, resp_parts, centroids, features):
+    cents, size = resp_parts[0].shape
+    rows, cols = features.shape
     tc = min(512, cols)
     return pl.pallas_call(
-        functools.partial(update_kernel, n_data, n_feat),
+        functools.partial(update_kernel, len(resp_parts)),
         grid=(cols // tc,),
-        in_specs=[
-            pl.BlockSpec(memory_space=pltpu.SMEM),
-            pl.BlockSpec(
-                (groups, cents, size), lambda j: (0, 0, 0), pipeline_mode=pl.Buffered(1)
-            ),
+        in_specs=[pl.BlockSpec(memory_space=pltpu.SMEM)]
+        + [
+            pl.BlockSpec((cents, size), lambda j: (0, 0), pipeline_mode=pl.Buffered(1))
+            for _ in resp_parts
+        ]
+        + [
             pl.BlockSpec((cents, tc), lambda j: (0, j)),
-        ]
-        + [pl.BlockSpec((depth, tc), lambda j: (0, j))] * n_data,
+            pl.BlockSpec((rows, tc), lambda j: (0, j)),
+        ],
         out_specs=pl.BlockSpec((cents, tc), lambda j: (0, j)),
         out_shape=jax.ShapeDtypeStruct((cents, cols), jnp.float32),
         scratch_shapes=[
@@ -166,7 +170,7 @@
             transcendentals=0,
         ),
         name="update",
-    )(order, resp, centroids, *features)
+    )(places, *resp_parts, centroids, features)
 
 
 def my_part(x, axis_name):
@@ -189,8 +193,10 @@
     halves = from_others(my_part(own, "feat"), "dp")
     wide = centroids.astype(jnp.float32)
     center_sq = jnp.sum(wide * wide, axis=1, keepdims=True)
-    own_features = featurize(own, projection, phases)
-    partial_value = score(centroids, own_features, center_sq, n_feat)
+    depth = own.shape[0]
+    total_rows = depth * n_data
+    features = featurize(own, projection, phases, total_rows, 0, None)
+    partial_value = score(centroids, features, center_sq, depth, n_feat)
     partial_value, *halves = lax.optimization_barrier((partial_value, *halves))
     others = [
         jnp.concatenate([half] + from_others(half, "feat"), axis=0) for half in halves
@@ -205,15 +211,19 @@
     peak = jnp.max(stats[:, 0], axis=0)
     norm = jnp.sum(stats[:, 1] * jnp.exp(stats[:, 0] - peak[None, :]), axis=0)
     resp = (jnp.exp(logits - peak[None, :]) / norm[None, :]).astype(jnp.bfloat16)
-    all_resp = lax.all_gather(resp, ("dp", "feat"), axis=0, tiled=False)
-    features = [own_features] + [featurize(x, projection, phases) for x in others]
-    order = [dp * n_feat + t for t in range(n_feat)] + [
-        (dp + n_data - s) % n_data * n_feat + (feat + n_feat - t) % n_feat
-        for s in range(1, n_data)
-        for t in range(n_feat)
-    ]
-    order = jnp.stack(order).astype(jnp.int32)
-    return update(order, all_resp, centroids, features, n_feat)
+    parts = [resp] + from_others(resp, "feat")
+    far = from_others(resp, "dp")
+    for s in range(1, n_data - 1):
+        features = featurize(others[s - 1], projection, phases, total_rows, s * depth, features)
+    features, *far = lax.optimization_barrier((features, *far))
+    for part in far:
+        parts += [part] + from_others(part, "feat")
+    s = n_data - 1
+    features = featurize(others[s - 1], projection, phases, total_rows, s * depth, features)
+    places = [(feat + n_feat - t) % n_feat for t in range(n_feat)]
+    places += [feat * 0 + g for g in range(n_feat, n_data * n_feat)]
+    places = jnp.stack(places).astype(jnp.int32)
+    return update(places, parts, centroids, features)
 
 
 def solution(mesh):

time: 213 us -> 236 us (1.11)
  waiting for transfers between devices: 30.7 us -> 56.9 us
  local copies, waits for them, and re-layouts: 25.5 us -> 15.9 us
  starting transfers between devices: 11 us -> 15 us
  Pallas kernels: 118 us -> 121 us
    ppermute x9 -> x16, waiting for transfers between devices: 3.48 us -> 31.2 us  [from_others(): lax.ppermute(x, axis_name, [(i, (i + s) % n) for i in range(n)])]
    unnamed x30 -> x38, local copies, waits for them, and re-layouts: 23.1 us -> 13.6 us
    ppermute x9 -> x16, starting transfers between devices: 10.9 us -> 14.9 us  [from_others(): lax.ppermute(x, axis_name, [(i, (i + s) % n) for i in range(n)])]
    pallas_call x5, Pallas kernels: 107 us -> 110 us  [the longest x4 65.9 us: featurize(): pl.pallas_call(lambda *refs: kernel(*refs[:3], refs[-1]), grid=(cols // t...]
  transfers between devices with their start and end apart: 12 -> 18, of which waited for: 4 -> 6; matrix products, arithmetic and copies ran while one was open for 5% -> 5% of each run, Pallas kernels for 35% -> 33%
where the time goes in v3:
time: 236 us
  Pallas kernels  121 us (51%)
  waiting for transfers between devices  56.9 us (24%)
  local copies, waits for them, and re-layouts  15.9 us (7%)
  starting transfers between devices  15 us (6%)
  between operations  13.6 us (6%)
  other arithmetic  13.5 us (6%)
    pallas_call x4, Pallas kernels, featurize(): pl.pallas_call(lambda *refs: kernel(*refs[:3], refs[-1]), grid=(cols // t...  65.9 us
    pallas_call x1, Pallas kernels, update(): pl.pallas_call(functools.partial(update_kernel, len(resp_parts)), grid=(c...  43.7 us
    ppermute x16, waiting for transfers between devices, from_others(): lax.ppermute(x, axis_name, [(i, (i + s) % n) for i in range(n)])  31.2 us
    all_gather x1, waiting for transfers between devices, shards(): lax.all_gather(my_part(embeddings, 'feat'), ('cent', 'feat'), axis=0, til...  23.2 us
    ppermute x16, starting transfers between devices, from_others(): lax.ppermute(x, axis_name, [(i, (i + s) % n) for i in range(n)])  14.9 us
    unnamed x38, local copies, waits for them, and re-layouts  13.6 us
    pallas_call x1, Pallas kernels, score(): pl.pallas_call(functools.partial(score_kernel, min(256, cents)), grid=(gr...  11.3 us
    concatenate x3, other arithmetic, shards(): jnp.concatenate([half] + from_others(half, 'feat'), axis=0)  5.61 us
  transfers between devices with their start and end apart: 18, of which 6 were waited for; matrix products, arithmetic and copies ran while one was open for 5% of the time, Pallas kernels for 33%

profile of v3, /device:TPU:0, one launch (start us, length us, event | category | flops | bytes accessed | tf_op | source)
XLA Modules:
  0.0 235.8 jit_solution(4492506365561847621)
XLA Ops:
  6.5 1.0 copy-done
  7.5 0.7 constant_dynamic-slice_fusion.1
  8.3 5.1 %multiply_reduce_fusion = f32[1024]{0:T(1024)S(1)} fusion(bf16[1024,4096]{1,0:T(8,128)(2,1)} %refs_8_.1), kind=kLoop, calls=%fused_computation | loop fusion | flops 12581888 | bytes 8392704 | tf_op jit(solution)/shard_map/reduce_sum | solution.py:195
  13.4 0.2 copy.11.s_ref
  13.6 23.2 %all-gather.2.cloned.1.call-done.refs_0_ = bf16[1024,768]{1,0:T(8,128)(2,1)} async-done(((bf16[128,768]{1,0:T(8,128)(2,1)}), bf16[1024,768]{1,0:T(8,128)(2,1)}) %all-gather.2.cloned.1.call-update) | async-done | bytes 1572880 | tf_op jit(solution)/shard_map/all_gather | solution.py:192
  36.8 1.2 constant_dynamic-slice_fusion
  38.0 2.4 %collective-permute-start.2 = (bf16[512,768]{1,0:T(8,128)(2,1)S(1)}, bf16[512,768]{1,0:T(8,128)(2,1)}, u32[]{:S(2)}, u32[]{:S(2)}) collective-permute-start(bf16[512,768]{1,0:T(8,128)(2,1)S(1)} %constant_dynamic-slice_fusion), channel_id=1, source_target_pairs={{0,24},{8,0},{16,8},{24,16},{1,25},{9,1},{17,9},{25,17},{2,26},{10... | collective-permute-start | bytes 2359304 | tf_op jit(solution)/shard_map/ppermute | solution.py:184
  40.4 0.6 collective-permute-start.1
  41.0 0.6 collective-permute-start
  41.5 2.8 %copy-done.2 = bf16[768,4096]{1,0:T(8,128)(2,1)S(1)} copy-done((bf16[768,4096]{1,0:T(8,128)(2,1)S(1)}, bf16[768,4096]{1,0:T(8,128)(2,1)}, u32[]{:S(2)}) %copy-start.2) | copy-done | bytes 6291480
  44.3 1.4 copy-done.7
  45.7 16.5 %featurize.4.f_ref.refs_3_ = bf16[4096,4096]{1,0:T(8,128)(2,1)} custom-call(bf16[1024,768]{1,0:T(8,128)(2,1)S(1)} %copy-done.7, bf16[768,4096]{1,0:T(8,128)(2,1)S(1)} %copy-done.2, f32[1,4096]{1,0:T(1,128)S(1)} %bitcast.23), custom_call_target="tpu_custom_call" | custom-call | flops 19327352832 | bytes 16252928 | tf_op jit(solution)/shard_map/featurize/pallas_call | solution.py:71
  62.2 11.3 %score.1 = f32[2,1024,512]{2,1,0:T(8,128)S(1)} custom-call(bf16[1024,4096]{1,0:T(8,128)(2,1)S(1)} %copy-done.4, bf16[4096,4096]{1,0:T(8,128)(2,1)} %featurize.4.f_ref.refs_3_, f32[1024,1]{1,0:T(8,128)S(1)} %copy.11.s_ref), custom_call_target="tpu_custom_call" | custom-call | flops 8589934592 | bytes 20971520 | tf_op jit(solution)/shard_map/score/pallas_call | solution.py:104
  73.5 2.0 copy-done.5
  75.5 1.2 collective-permute-done.1
  76.7 0.1 collective-permute-start.3
  76.8 0.8 copy-done.10
  77.6 0.5 collective-permute-start.5
  78.1 0.1 stack.35.i_ref
  78.2 1.0 collective-permute-done.3
  79.2 2.4 %pad_maximum_fusion.refs_0_ = bf16[1024,768]{1,0:T(8,128)(2,1)} fusion(bf16[512,768]{1,0:T(8,128)(2,1)} %collective-permute-done.3, bf16[512,768]{1,0:T(8,128)(2,1)S(1)} %collective-permute-done), kind=kLoop, calls=%fused_computation.4 | loop fusion | flops 3145728 | bytes 3145728 | tf_op jit(solution)/shard_map/concatenate | solution.py:202
  81.6 1.2 pad_maximum_fusion.1.refs_0_
  82.9 2.0 pad_maximum_fusion.2.refs_0_
  84.8 2.5 %reduce-scatter.2.cloned.1.call-done = f32[1,1024,512]{2,1,0:T(8,128)} async-done(((f32[2,1024,512]{2,1,0:T(8,128)}), f32[1,1024,512]{2,1,0:T(8,128)}) %reduce-scatter.2.cloned.1.call-update) | async-done | bytes 2097168 | tf_op jit(solution)/shard_map/reduce_scatter | solution.py:204
  87.3 2.0 multiply_reduce_fusion.1
  89.3 0.2 copy-done.9
  89.5 0.4 exponential_reduce_fusion
  90.0 2.8 %collective-permute-start.7 = (f32[2,512]{1,0:T(2,128)S(1)}, f32[2,512]{1,0:T(2,128)S(1)}, u32[]{:S(2)}, u32[]{:S(2)}) collective-permute-start(f32[2,512]{1,0:T(2,128)S(1)} %get-tuple-element.30), channel_id=1, source_target_pairs={{0,2},{1,3},{2,0},{3,1},{4,6},{5,7},{6,4},{7,5},{8,10},{9,11},{10,... | collective-permute-start | bytes 12296 | tf_op jit(solution)/shard_map/ppermute | solution.py:184
  92.7 1.5 collective-permute-start.6
  94.2 2.4 %collective-permute-start.8 = (f32[2,512]{1,0:T(2,128)S(1)}, f32[2,512]{1,0:T(2,128)S(1)}, u32[]{:S(2)}, u32[]{:S(2)}) collective-permute-start(f32[2,512]{1,0:T(2,128)S(1)} %get-tuple-element.30), channel_id=1, source_target_pairs={{0,3},{1,0},{2,1},{3,2},{4,7},{5,4},{6,5},{7,6},{8,11},{9,8},{10,9... | collective-permute-start | bytes 12296 | tf_op jit(solution)/shard_map/ppermute | solution.py:184
  96.6 2.8 %copy-done.3 = bf16[768,4096]{1,0:T(8,128)(2,1)S(1)} copy-done((bf16[768,4096]{1,0:T(8,128)(2,1)S(1)}, bf16[768,4096]{1,0:T(8,128)(2,1)}, u32[]{:S(2)}) %copy-start.3) | copy-done | bytes 6291480
  99.3 16.5 %featurize.5.refs_3_ = bf16[4096,4096]{1,0:T(8,128)(2,1)} custom-call(bf16[1024,768]{1,0:T(8,128)(2,1)S(1)} %copy-done.6, bf16[768,4096]{1,0:T(8,128)(2,1)S(1)} %copy-done.3, f32[1,4096]{1,0:T(1,128)S(1)} %bitcast.24, bf16[4096,4096]{1,0:T(8,128)(2,1)} %featurize.4.f_ref.refs_3_), custom_call_target="tpu_custom_call", output_to_operand_aliasing={{}: (3, {})} | custom-call | flops 19327352832 | bytes 16252928 | tf_op jit(solution)/shard_map/featurize/pallas_call | solution.py:71
  116.0 0.4 divide_convert_fusion.refs_0_
  116.3 2.4 %collective-permute-start.12 = (bf16[1024,512]{1,0:T(8,128)(2,1)S(1)}, bf16[1024,512]{1,0:T(8,128)(2,1)S(1)}, u32[]{:S(2)}, u32[]{:S(2)}) collective-permute-start(bf16[1024,512]{1,0:T(8,128)(2,1)S(1)} %divide_convert_fusion.refs_0_), channel_id=1, source_target_pairs={{0,24},{8,0},{16,8},{24,16},{1,25},{9,1},{17,9},{25,17},{2,26},{10... | collective-permute-start | bytes 3145736 | tf_op jit(solution)/shard_map/ppermute | solution.py:184
  118.8 0.5 collective-permute-start.11
  119.3 0.6 collective-permute-start.10
  119.9 16.5 %featurize.6.refs_3_ = bf16[4096,4096]{1,0:T(8,128)(2,1)} custom-call(bf16[1024,768]{1,0:T(8,128)(2,1)S(1)} %pad_maximum_fusion.1.refs_0_, bf16[768,4096]{1,0:T(8,128)(2,1)S(1)} %copy-done.3, f32[1,4096]{1,0:T(1,128)S(1)} %bitcast.25, bf16[4096,4096]{1,0:T(8,128)(2,1)} %featurize.5.refs_3_), custom_call_target="tpu_custom_call", output_to_operand_aliasing={{}: (3, {})} | custom-call | flops 19327352832 | bytes 16252928 | tf_op jit(solution)/shard_map/featurize/pallas_call | solution.py:71
  136.4 6.1 %collective-permute-done.12.refs_6_ = bf16[1024,512]{1,0:T(8,128)(2,1)S(1)} collective-permute-done((bf16[1024,512]{1,0:T(8,128)(2,1)S(1)}, bf16[1024,512]{1,0:T(8,128)(2,1)S(1)}, u32[]{:S(2)}, u32[]{:S(2)}) %collective-permute-start.12) | collective-permute-done | bytes 1048608 | tf_op jit(solution)/shard_map/ppermute | solution.py:184
  142.5 22.9 %collective-permute-done.11.refs_4_ = bf16[1024,512]{1,0:T(8,128)(2,1)S(1)} collective-permute-done((bf16[1024,512]{1,0:T(8,128)(2,1)S(1)}, bf16[1024,512]{1,0:T(8,128)(2,1)S(1)}, u32[]{:S(2)}, u32[]{:S(2)}) %collective-permute-start.11) | collective-permute-done | bytes 1048608 | tf_op jit(solution)/shard_map/ppermute | solution.py:184
  165.4 0.1 collective-permute-start.13
  165.5 0.5 collective-permute-start.14
  166.0 0.1 collective-permute-start.15
  166.0 16.5 %featurize.7.refs_9_ = bf16[4096,4096]{1,0:T(8,128)(2,1)} custom-call(bf16[1024,768]{1,0:T(8,128)(2,1)S(1)} %pad_maximum_fusion.2.refs_0_, bf16[768,4096]{1,0:T(8,128)(2,1)S(1)} %copy-done.3, f32[1,4096]{1,0:T(1,128)S(1)} %bitcast.26, bf16[4096,4096]{1,0:T(8,128)(2,1)} %featurize.6.refs_3_), custom_call_target="tpu_custom_call", output_to_operand_aliasing={{}: (3, {})} | custom-call | flops 19327352832 | bytes 16252928 | tf_op jit(solution)/shard_map/featurize/pallas_call | solution.py:71
  182.6 0.9 copy-done.15
  183.5 0.3 copy-done.16
  183.9 0.3 copy-done.17
  184.2 1.0 copy-done.18
  185.2 43.7 %update.1 = f32[1024,4096]{1,0:T(8,128)} custom-call(s32[8]{0:T(128)S(1)} %stack.35.i_ref, bf16[1024,512]{1,0:T(8,128)(2,1)S(1)} %divide_convert_fusion.refs_0_, bf16[1024,512]{1,0:T(8,128)(2,1)} %copy-done.15, bf16[1024,512]{1,0:T(8,128)(2,1)} %copy-done.14, bf16[1024,512]{1,0:T(8,128)(2,1)} %copy-done.16, bf16[1024,512]{1,0:T(8,128)(2,1)} %copy-done.13, ...), custom_call_target="tpu_custom_call" | custom-call | flops 34359738368 | bytes 67108864 | tf_op jit(solution)/shard_map/update/pallas_call | solution.py:148
  (53 shorter events, 0.3 us)
Async XLA Ops:
  6.5 1.0 copy-start
  6.5 30.2 %all-gather.2.cloned.1.call-start = ((), (), s32[]{:S(2)}) async-start(), calls=%async_computation.1 | async-start | bytes 1769472 | tf_op jit(solution)/shard_map/all_gather | solution.py:192
  8.2 79.1 %reduce-scatter.2.cloned.1.call-start = ((), (), s32[]{:S(2)}) async-start(), calls=%async_computation.2 | async-start | bytes 6291456 | tf_op jit(solution)/shard_map/reduce_scatter | solution.py:204
  13.4 28.2 %copy-start.8 = (f32[4096]{0:T(1024)S(1)}, f32[4096]{0:T(1024)}, u32[]{:S(2)}) copy-start(f32[4096]{0:T(1024)} %param.6) | copy-start | bytes 49156
  38.0 37.5 %collective-permute-start.2 = (bf16[512,768]{1,0:T(8,128)(2,1)S(1)}, bf16[512,768]{1,0:T(8,128)(2,1)}, u32[]{:S(2)}, u32[]{:S(2)}) collective-permute-start(bf16[512,768]{1,0:T(8,128)(2,1)S(1)} %constant_dynamic-slice_fusion), channel_id=1, source_target_pairs={{0,24},{8,0},{16,8},{24,16},{1,25},{9,1},{17,9},{25,17},{2,26},{10... | collective-permute-start | bytes 2359304 | tf_op jit(solution)/shard_map/ppermute | solution.py:184
  40.4 36.3 %collective-permute-start.1 = (bf16[512,768]{1,0:T(8,128)(2,1)S(1)}, bf16[512,768]{1,0:T(8,128)(2,1)S(1)}, u32[]{:S(2)}, u32[]{:S(2)}) collective-permute-start(bf16[512,768]{1,0:T(8,128)(2,1)S(1)} %constant_dynamic-slice_fusion), channel_id=1, source_target_pairs={{0,16},{8,24},{16,0},{24,8},{1,17},{9,25},{17,1},{25,9},{2,18},{10... | collective-permute-start | bytes 2359304 | tf_op jit(solution)/shard_map/ppermute | solution.py:184
  41.0 35.7 %collective-permute-start = (bf16[512,768]{1,0:T(8,128)(2,1)S(1)}, bf16[512,768]{1,0:T(8,128)(2,1)S(1)}, u32[]{:S(2)}, u32[]{:S(2)}) collective-permute-start(bf16[512,768]{1,0:T(8,128)(2,1)S(1)} %constant_dynamic-slice_fusion), channel_id=1, source_target_pairs={{0,8},{8,16},{16,24},{24,0},{1,9},{9,17},{17,25},{25,1},{2,10},{10... | collective-permute-start | bytes 2359304 | tf_op jit(solution)/shard_map/ppermute | solution.py:184
  41.5 2.8 %copy-start.2 = (bf16[768,4096]{1,0:T(8,128)(2,1)S(1)}, bf16[768,4096]{1,0:T(8,128)(2,1)}, u32[]{:S(2)}) copy-start(bf16[768,4096]{1,0:T(8,128)(2,1)} %refs_1_.7) | copy-start | bytes 18874372
  44.3 1.4 copy-start.7
  45.7 16.5 %copy-start.4 = (bf16[1024,4096]{1,0:T(8,128)(2,1)S(1)}, bf16[1024,4096]{1,0:T(8,128)(2,1)}, u32[]{:S(2)}) copy-start(bf16[1024,4096]{1,0:T(8,128)(2,1)} %refs_8_.1) | copy-start | bytes 25165828
  73.5 2.0 copy-start.5
  76.7 0.9 copy-start.10
  76.7 2.5 %collective-permute-start.3 = (bf16[512,768]{1,0:T(8,128)(2,1)S(1)}, bf16[512,768]{1,0:T(8,128)(2,1)}, u32[]{:S(2)}, u32[]{:S(2)}) collective-permute-start(bf16[512,768]{1,0:T(8,128)(2,1)S(1)} %collective-permute-done), channel_id=1, source_target_pairs={{0,4},{4,0},{1,5},{5,1},{2,6},{6,2},{3,7},{7,3},{8,12},{12,8},{9,1... | collective-permute-start | bytes 2359304 | tf_op jit(solution)/shard_map/ppermute | solution.py:184
  77.6 4.0 %collective-permute-start.4 = (bf16[512,768]{1,0:T(8,128)(2,1)S(1)}, bf16[512,768]{1,0:T(8,128)(2,1)}, u32[]{:S(2)}, u32[]{:S(2)}) collective-permute-start(bf16[512,768]{1,0:T(8,128)(2,1)S(1)} %collective-permute-done.1), channel_id=1, source_target_pairs={{0,4},{4,0},{1,5},{5,1},{2,6},{6,2},{3,7},{7,3},{8,12},{12,8},{9,1... | collective-permute-start | bytes 2359304 | tf_op jit(solution)/shard_map/ppermute | solution.py:184
  77.6 4.0 %copy-start.11 = (bf16[512,768]{1,0:T(8,128)(2,1)S(1)}, bf16[512,768]{1,0:T(8,128)(2,1)}, u32[]{:S(2)}) copy-start(bf16[512,768]{1,0:T(8,128)(2,1)} %copy-done.10) | copy-start | bytes 2359300
  77.6 5.3 %collective-permute-start.5 = (bf16[512,768]{1,0:T(8,128)(2,1)}, bf16[512,768]{1,0:T(8,128)(2,1)}, u32[]{:S(2)}, u32[]{:S(2)}) collective-permute-start(bf16[512,768]{1,0:T(8,128)(2,1)} %collective-permute-done.2), channel_id=1, source_target_pairs={{0,4},{4,0},{1,5},{5,1},{2,6},{6,2},{3,7},{7,3},{8,12},{12,8},{9,1... | collective-permute-start | bytes 2359304 | tf_op jit(solution)/shard_map/ppermute | solution.py:184
  87.3 2.2 copy-start.9
  87.3 9.2 %copy-start.6 = (bf16[1024,768]{1,0:T(8,128)(2,1)S(1)}, bf16[1024,768]{1,0:T(8,128)(2,1)}, u32[]{:S(2)}) copy-start(bf16[1024,768]{1,0:T(8,128)(2,1)} %pad_maximum_fusion.refs_0_) | copy-start | bytes 4718596
  90.0 25.9 %collective-permute-start.7 = (f32[2,512]{1,0:T(2,128)S(1)}, f32[2,512]{1,0:T(2,128)S(1)}, u32[]{:S(2)}, u32[]{:S(2)}) collective-permute-start(f32[2,512]{1,0:T(2,128)S(1)} %get-tuple-element.30), channel_id=1, source_target_pairs={{0,2},{1,3},{2,0},{3,1},{4,6},{5,7},{6,4},{7,5},{8,10},{9,11},{10,... | collective-permute-start | bytes 12296 | tf_op jit(solution)/shard_map/ppermute | solution.py:184
  92.7 23.1 %collective-permute-start.6 = (f32[2,512]{1,0:T(2,128)S(1)}, f32[2,512]{1,0:T(2,128)S(1)}, u32[]{:S(2)}, u32[]{:S(2)}) collective-permute-start(f32[2,512]{1,0:T(2,128)S(1)} %get-tuple-element.30), channel_id=1, source_target_pairs={{0,1},{1,2},{2,3},{3,0},{4,5},{5,6},{6,7},{7,4},{8,9},{9,10},{10,1... | collective-permute-start | bytes 12296 | tf_op jit(solution)/shard_map/ppermute | solution.py:184
  94.2 21.7 %collective-permute-start.8 = (f32[2,512]{1,0:T(2,128)S(1)}, f32[2,512]{1,0:T(2,128)S(1)}, u32[]{:S(2)}, u32[]{:S(2)}) collective-permute-start(f32[2,512]{1,0:T(2,128)S(1)} %get-tuple-element.30), channel_id=1, source_target_pairs={{0,3},{1,0},{2,1},{3,2},{4,7},{5,4},{6,5},{7,6},{8,11},{9,8},{10,9... | collective-permute-start | bytes 12296 | tf_op jit(solution)/shard_map/ppermute | solution.py:184
  96.6 2.8 %copy-start.3 = (bf16[768,4096]{1,0:T(8,128)(2,1)S(1)}, bf16[768,4096]{1,0:T(8,128)(2,1)}, u32[]{:S(2)}) copy-start(bf16[768,4096]{1,0:T(8,128)(2,1)} %refs_1_.7) | copy-start | bytes 18874372
  116.3 26.1 %collective-permute-start.12 = (bf16[1024,512]{1,0:T(8,128)(2,1)S(1)}, bf16[1024,512]{1,0:T(8,128)(2,1)S(1)}, u32[]{:S(2)}, u32[]{:S(2)}) collective-permute-start(bf16[1024,512]{1,0:T(8,128)(2,1)S(1)} %divide_convert_fusion.refs_0_), channel_id=1, source_target_pairs={{0,24},{8,0},{16,8},{24,16},{1,25},{9,1},{17,9},{25,17},{2,26},{10... | collective-permute-start | bytes 3145736 | tf_op jit(solution)/shard_map/ppermute | solution.py:184
  118.8 46.6 %collective-permute-start.11 = (bf16[1024,512]{1,0:T(8,128)(2,1)S(1)}, bf16[1024,512]{1,0:T(8,128)(2,1)S(1)}, u32[]{:S(2)}, u32[]{:S(2)}) collective-permute-start(bf16[1024,512]{1,0:T(8,128)(2,1)S(1)} %divide_convert_fusion.refs_0_), channel_id=1, source_target_pairs={{0,16},{8,24},{16,0},{24,8},{1,17},{9,25},{17,1},{25,9},{2,18},{10... | collective-permute-start | bytes 3145736 | tf_op jit(solution)/shard_map/ppermute | solution.py:184
  119.3 46.1 %collective-permute-start.10 = (bf16[1024,512]{1,0:T(8,128)(2,1)S(1)}, bf16[1024,512]{1,0:T(8,128)(2,1)S(1)}, u32[]{:S(2)}, u32[]{:S(2)}) collective-permute-start(bf16[1024,512]{1,0:T(8,128)(2,1)S(1)} %divide_convert_fusion.refs_0_), channel_id=1, source_target_pairs={{0,8},{8,16},{16,24},{24,0},{1,9},{9,17},{17,25},{25,1},{2,10},{10... | collective-permute-start | bytes 3145736 | tf_op jit(solution)/shard_map/ppermute | solution.py:184
  136.4 46.2 %collective-permute-start.9 = (bf16[1024,512]{1,0:T(8,128)(2,1)S(1)}, bf16[1024,512]{1,0:T(8,128)(2,1)S(1)}, u32[]{:S(2)}, u32[]{:S(2)}) collective-permute-start(bf16[1024,512]{1,0:T(8,128)(2,1)S(1)} %divide_convert_fusion.refs_0_), channel_id=1, source_target_pairs={{0,4},{4,0},{1,5},{5,1},{2,6},{6,2},{3,7},{7,3},{8,12},{12,8},{9,1... | collective-permute-start | bytes 3145736 | tf_op jit(solution)/shard_map/ppermute | solution.py:184
  142.5 40.0 %copy-start.12 = (bf16[1024,512]{1,0:T(8,128)(2,1)}, bf16[1024,512]{1,0:T(8,128)(2,1)S(1)}, u32[]{:S(2)}) copy-start(bf16[1024,512]{1,0:T(8,128)(2,1)S(1)} %collective-permute-done.12.refs_6_) | copy-start | bytes 3145732
  165.4 17.1 %copy-start.13 = (bf16[1024,512]{1,0:T(8,128)(2,1)}, bf16[1024,512]{1,0:T(8,128)(2,1)S(1)}, u32[]{:S(2)}) copy-start(bf16[1024,512]{1,0:T(8,128)(2,1)S(1)} %collective-permute-done.11.refs_4_) | copy-start | bytes 3145732
  165.4 17.1 %copy-start.14 = (bf16[1024,512]{1,0:T(8,128)(2,1)}, bf16[1024,512]{1,0:T(8,128)(2,1)S(1)}, u32[]{:S(2)}) copy-start(bf16[1024,512]{1,0:T(8,128)(2,1)S(1)} %collective-permute-done.10.refs_2_) | copy-start | bytes 3145732
  165.4 17.2 %collective-permute-start.13 = (bf16[1024,512]{1,0:T(8,128)(2,1)S(1)}, bf16[1024,512]{1,0:T(8,128)(2,1)S(1)}, u32[]{:S(2)}, u32[]{:S(2)}) collective-permute-start(bf16[1024,512]{1,0:T(8,128)(2,1)S(1)} %collective-permute-done.10.refs_2_), channel_id=1, source_target_pairs={{0,4},{4,0},{1,5},{5,1},{2,6},{6,2},{3,7},{7,3},{8,12},{12,8},{9,1... | collective-permute-start | bytes 3145736 | tf_op jit(solution)/shard_map/ppermute | solution.py:184
  165.5 17.1 %collective-permute-start.14 = (bf16[1024,512]{1,0:T(8,128)(2,1)S(1)}, bf16[1024,512]{1,0:T(8,128)(2,1)S(1)}, u32[]{:S(2)}, u32[]{:S(2)}) collective-permute-start(bf16[1024,512]{1,0:T(8,128)(2,1)S(1)} %collective-permute-done.11.refs_4_), channel_id=1, source_target_pairs={{0,4},{4,0},{1,5},{5,1},{2,6},{6,2},{3,7},{7,3},{8,12},{12,8},{9,1... | collective-permute-start | bytes 3145736 | tf_op jit(solution)/shard_map/ppermute | solution.py:184
  166.0 16.6 %collective-permute-start.15 = (bf16[1024,512]{1,0:T(8,128)(2,1)S(1)}, bf16[1024,512]{1,0:T(8,128)(2,1)S(1)}, u32[]{:S(2)}, u32[]{:S(2)}) collective-permute-start(bf16[1024,512]{1,0:T(8,128)(2,1)S(1)} %collective-permute-done.12.refs_6_), channel_id=1, source_target_pairs={{0,4},{4,0},{1,5},{5,1},{2,6},{6,2},{3,7},{7,3},{8,12},{12,8},{9,1... | collective-permute-start | bytes 3145736 | tf_op jit(solution)/shard_map/ppermute | solution.py:184
  182.5 1.0 copy-start.15
  182.6 1.3 copy-start.16
  182.6 1.6 copy-start.17
  184.2 1.0 copy-start.18
  185.2 43.7 %copy-start.1 = (bf16[256,768]{1,0:T(8,128)(2,1)S(1)}, bf16[256,768]{1,0:T(8,128)(2,1)}, u32[]{:S(2)}) copy-start(bf16[256,768]{1,0:T(8,128)(2,1)} %param.4) | copy-start | bytes 1179652
Sparse Core Ops, SparseCore 0:
  9.0 27.7 all-gather.1
  76.8 10.4 reduce-scatter.1
